TPU v7x, 32 devices: a whole 2x2x4 slice. The times are simulated.
32 devices in a mesh: groups: 2 (over y), seq: 16 (over z, x, core).
Axes of the slice: x: 2, y: 2, z: 4, core: 2. Of those that a mesh axis runs over, the one named last changes fastest.
Arguments:
- tokens: bfloat16 [8192, 4096], P(('groups', 'seq')), parts along dimension 0, may hold values from -6 to 6
- input_norm_scale: float32 [4096], replicated, may hold values from 0.1 to 1.9
- key_matrix: bfloat16 [4096, 1024], replicated, may hold values from -0.09375 to 0.09375
- adapter_down_weight: bfloat16 [32, 4096, 64], P('seq'), may hold values from -0.09375 to 0.09375
- adapter_up_weight: bfloat16 [32, 64, 1024], P('seq'), may hold values from -0.75 to 0.75
- lengths: int32 [16], P('groups'), parts along dimension 0, may hold values from 1 to 1024, 4096 in all
- prompt_adapter_index: int32 [16, 1], P('groups'), parts along dimension 0, may hold values from 0 to 7
- active_adapter_ids: int32 [16], P('groups'), parts along dimension 0, may hold values from 0 to 31, as said below
- token_cache_device: int32 [8192, 1], P(('groups', 'seq')), parts along dimension 0, may hold values from 0 to 15; in each aligned block of 256 rows (0 to 255, 256 to 511, ...) at most 32 rows name the same one
Outputs:
- key_cache: bfloat16 [16384, 1024], P(('groups', 'seq')), parts along dimension 0
There are 2 independent parts, one for each index of `groups`. A program takes and returns all parts, laid end to end along the dimension named above; an argument that names none is the same for every part. Nothing has to cross between parts.
Inputs may be any that keep to these rules, and one draw needn't show every extreme that they name: `active_adapter_ids`: distinct store ids; adapter a is held by device a // 2 of seq in its slot a % 2. `prompt_adapter_index`: every index is used by some prompt. `lengths`: the 4096 rows hold the prompts end to end. `token_cache_device`: the rows of one device name any one device at most 32 times.
All inputs are finite; a program needn't handle non-finite values.
Results may differ from a plain program's by a relative error of at most 0.0054.
Values may be sent and summed in bfloat16 or wider, within the bound.
No kernel may reach another device: no remote copies, remote signals or barrier semaphores. Data moves between devices by JAX's collectives and lax.ppermute only.
A program may use at most 128 MiB of HBM per device.

v0:
```python
import functools

import jax
import jax.numpy as jnp
from jax import lax
from jax.experimental import pallas as pl
from jax.experimental.pallas import tpu as pltpu
from jax.sharding import PartitionSpec as P

HEAD = 128
ADAPTER_RANK = 64


rope_theta = 500000.0
norm_eps = 1e-05


def spread(array, axis, root):
    mine = lax.axis_index(axis) == root
    return lax.psum(jnp.where(mine, array, jnp.zeros_like(array)), axis)


def rotate(projected, positions):
    half_head = HEAD // 2
    frequencies = rope_theta ** (-(jnp.arange(half_head, dtype=jnp.float32) * 2.0) / HEAD)
    angles = positions.astype(jnp.float32)[:, None] * frequencies[None, :]
    cosine = jnp.cos(angles)[:, None, :]
    sine_table = jnp.sin(angles)[:, None, :]
    per_head = projected.reshape(projected.shape[0], -1, HEAD)
    first_half = per_head[..., :half_head]
    second_half = per_head[..., half_head:]
    turned = jnp.concatenate(
        [
            first_half * cosine - second_half * sine_table,
            second_half * cosine + first_half * sine_table,
        ],
        axis=-1,
    )
    return turned.reshape(projected.shape)


def locate(lengths, prompt_adapter_index, first_row, row_count):
    prompt_ends = jnp.cumsum(lengths)
    prompt_starts = prompt_ends - lengths
    row_ids = first_row + jnp.arange(row_count, dtype=jnp.int32)
    prompt_ids = jnp.sum((prompt_ends[None, :] <= row_ids[:, None]).astype(jnp.int32), axis=1)
    prompt_match = prompt_ids[:, None] == jnp.arange(lengths.shape[0], dtype=jnp.int32)[None, :]
    prompt_start = jnp.sum(jnp.where(prompt_match, prompt_starts[None, :], 0), axis=1)
    hot_slots = jnp.sum(jnp.where(prompt_match, prompt_adapter_index[:, 0][None, :], 0), axis=1)
    return (row_ids - prompt_start, hot_slots)


PLANE = 4
PLANES = 4
SLOT_CASES = ((2, 1, 1), (3, 2, 1), (3, 1, 2), (3, 2, 2), (3, 3, 1), (3, 1, 3), (4, 3, 3))
FEW = 4
ANY = pl.BlockSpec(memory_space=pl.ANY)
SMEM = pl.BlockSpec(memory_space=pltpu.SMEM)
VMEM = pl.BlockSpec(memory_space=pltpu.VMEM)
VMEM_LIMIT = 40 * 1024 * 1024


def swap(value, distance, peer_count):
    return lax.ppermute(value, "seq", [(i, i ^ distance) for i in range(peer_count)])


def call(kernel, out_shape, in_specs, out_specs, scratch=(), **cost):
    return pl.pallas_call(
        kernel,
        out_shape=out_shape,
        in_specs=in_specs,
        out_specs=out_specs,
        scratch_shapes=list(scratch),
        compiler_params=pltpu.CompilerParams(vmem_limit_bytes=VMEM_LIMIT),
        cost_estimate=pl.CostEstimate(transcendentals=0, **cost) if cost else None,
    )


FROM_KIND, FROM_SLOT, PLANE_LIST, DEVICE_LISTS, SECTIONS = 3, 4, 5, 6, 10


def bit_of(mask, entry):
    return lax.shift_right_logical(mask, entry) & 1


def plan_kernel(rows, adapter_device, length_ref, index_ref, id_ref, plan_ref):
    hot_count = id_ref.shape[0]
    device = lax.axis_index("seq")
    plane = lax.div(device, PLANE)
    place = device - plane * PLANE
    for at in range(FROM_KIND * hot_count):
        plan_ref[at] = 0
    for at in range(PLANE_LIST * hot_count, SECTIONS * hot_count):
        plan_ref[at] = -1
    devices = PLANE * PLANES
    uses = [jnp.int32(0)] * devices
    start = jnp.int32(0)
    for prompt in range(length_ref.shape[0]):
        end = start + length_ref[prompt]
        bit = lax.shift_left(jnp.int32(1), index_ref[prompt])
        plan_ref[SECTIONS * hot_count + 3 + 2 * prompt] = end
        plan_ref[SECTIONS * hot_count + 4 + 2 * prompt] = index_ref[prompt]
        for at in range(devices):
            hit = (start < (at + 1) * rows) & (end > at * rows)
            uses[at] = uses[at] | jnp.where(hit, bit, 0)
        start = end
    need = []
    for at in range(PLANES):
        mask = uses[at * PLANE]
        for inner in range(1, PLANE):
            mask = mask | uses[at * PLANE + inner]
        need.append(mask)

    def pick(masks, which):
        total = masks[0]
        for at in range(1, len(masks)):
            total = jnp.where(which == at, masks[at], total)
        return total

    def list_bits(section, mask, values):
        count = jnp.int32(0)
        for entry in range(hot_count):

            @pl.when(bit_of(mask, entry) == 1)
            def _():
                plan_ref[section * hot_count + count] = values[entry]

            count = count + bit_of(mask, entry)
        return count

    owner_plane = []
    kind = []
    slot = []
    local = []
    for entry in range(hot_count):
        adapter = id_ref[entry]
        owner = lax.div(adapter, adapter_device)
        owner_plane.append(lax.div(owner, PLANE))
        local.append(
            ((owner - owner_plane[entry] * PLANE) ^ place) * adapter_device
            + adapter
            - owner * adapter_device
        )
        kind.append(jnp.int32(0))
        slot.append(local[entry])
    need_here = pick(need, plane)
    for distance in range(1, PLANES):
        other = plane ^ distance
        need_there = pick(need, other)
        sent = jnp.int32(0)
        taken = jnp.int32(0)
        for entry in range(hot_count):
            plan_ref[(distance - 1) * hot_count + sent] = local[entry]
            sent = sent + jnp.where(owner_plane[entry] == plane, bit_of(need_there, entry), 0)
            wanted = jnp.where(owner_plane[entry] == other, bit_of(need_here, entry), 0)
            kind[entry] = jnp.where(wanted == 1, distance, kind[entry])
            slot[entry] = jnp.where(wanted == 1, taken, slot[entry])
            taken = taken + wanted
    for entry in range(hot_count):
        plan_ref[FROM_KIND * hot_count + entry] = kind[entry]
        plan_ref[FROM_SLOT * hot_count + entry] = slot[entry]
    listed = [jnp.int32(0)]
    for entry in range(hot_count):
        listed.append(listed[entry] + bit_of(need_here, entry))
    plan_ref[SECTIONS * hot_count] = list_bits(
        PLANE_LIST, need_here, [jnp.int32(entry) for entry in range(hot_count)]
    )
    for distance in range(PLANE):
        list_bits(DEVICE_LISTS + distance, pick(uses, device ^ distance), listed)
    most = []
    for distance in range(1, PLANES):
        largest = jnp.int32(0)
        for at in range(PLANES):
            count = jnp.int32(0)
            for entry in range(hot_count):
                wanted = bit_of(need[at ^ distance], entry)
                count = count + jnp.where(owner_plane[entry] == at, wanted, 0)
            largest = jnp.maximum(largest, count)
        most.append(largest)
    few = jnp.bool_(True)
    for at in range(devices):
        count = jnp.int32(0)
        for entry in range(hot_count):
            count = count + bit_of(uses[at], entry)
        few = few & (count <= FEW)
    case = jnp.int32(len(SLOT_CASES))
    for at in reversed(range(len(SLOT_CASES))):
        fits = jnp.bool_(True)
        for distance in range(PLANES - 1):
            fits = fits & (most[distance] <= SLOT_CASES[at][distance])
        case = jnp.where(fits, at, case)
    plan_ref[SECTIONS * hot_count + 1] = case
    plan_ref[SECTIONS * hot_count + 2] = jnp.where(few, 1, 0)


def norm_kernel(token_ref, scale_ref, out_ref, *quarter_refs):
    values = token_ref[...].astype(jnp.float32)
    inverse_rms = lax.rsqrt(jnp.mean(values * values, axis=1, keepdims=True) + norm_eps)
    out_ref[...] = (values * inverse_rms * scale_ref[...]).astype(jnp.bfloat16)
    place = lax.rem(lax.axis_index("seq"), PLANE)
    quarter = quarter_refs[0].shape[1]
    for distance in range(PLANE):
        first = pl.multiple_of((place ^ distance) * quarter, quarter)
        quarter_refs[distance][...] = out_ref[:, pl.ds(first, quarter)]


def pack_kernel(quarter, down_ref, up_ref, *refs):
    outs = refs[:PLANE]
    sems = refs[PLANE]
    place = lax.rem(lax.axis_index("seq"), PLANE)
    rank = down_ref.shape[1]
    part = rank // PLANE
    copies = []
    for distance in range(PLANE):
        other = place ^ distance
        columns = pl.ds(pl.multiple_of(other * quarter, quarter), quarter)
        copies.append(
            pltpu.make_async_copy(
                down_ref.at[:, :, columns],
                outs[distance].at[:, pl.ds(0, rank), :],
                sems.at[2 * distance],
            )
        )
        rows = pl.ds(pl.multiple_of(other * part, part), part)
        copies.append(
            pltpu.make_async_copy(
                up_ref.at[:, rows, :],
                outs[distance].at[:, pl.ds(rank, part), :],
                sems.at[2 * distance + 1],
            )
        )
    for copy in copies:
        copy.start()
    for copy in copies:
        copy.wait()


def select_kernel(slots, hot_count, adapter_device, plan_ref, *refs):
    local = refs[:PLANE]
    outs = refs[PLANE : PLANE + PLANES - 1]
    sems = refs[-1]
    waits = []
    for distance in range(1, PLANES):
        for slot in range(slots[distance - 1]):
            index = plan_ref[(distance - 1) * hot_count + slot]
            holder = lax.div(index, adapter_device)
            inner = index - holder * adapter_device
            target = outs[distance - 1].at[slot]
            sem = sems.at[len(waits)]
            for at in range(PLANE):

                @pl.when(holder == at)
                def _():
                    pltpu.make_async_copy(local[at].at[inner], target, sem).start()

            waits.append(pltpu.make_async_copy(local[0].at[0], target, sem))
    for wait in waits:
        wait.wait()


def start_rows(plan_ref, entry, hot_count, adapter_device, local, arrived, copy_of):
    kind = plan_ref[FROM_KIND * hot_count + entry]
    slot = plan_ref[FROM_SLOT * hot_count + entry]

    @pl.when(kind == 0)
    def _():
        holder = lax.div(slot, adapter_device)
        inner = slot - holder * adapter_device
        for at in range(PLANE):

            @pl.when(holder == at)
            def _():
                copy_of(local[at].at[inner]).start()

    for distance in range(1, PLANES):

        @pl.when(kind == distance)
        def _():
            copy_of(arrived[distance - 1].at[slot]).start()


def share_rows(first, rank, hot_count, plan_ref, rows_ref, outs):
    for distance in range(PLANE):
        for at in range(outs[0].shape[0]):
            listed = plan_ref[(DEVICE_LISTS + distance) * hot_count + first + at]
            outs[distance][at] = rows_ref[jnp.maximum(listed, 0), rank:, :]


def share_kernel(first, rank, hot_count, plan_ref, rows_ref, *outs):
    share_rows(first, rank, hot_count, plan_ref, rows_ref, outs)


def collect_kernel(rank, hot_count, adapter_device, plan_ref, *refs):
    local = refs[:PLANE]
    arrived = refs[PLANE : PLANE + PLANES - 1]
    out_ref, *shares, sems = refs[PLANE + PLANES - 1 :]
    used = plan_ref[SECTIONS * hot_count]

    def copy_of(at):
        return lambda source: pltpu.make_async_copy(source, out_ref.at[at], sems.at[at])

    for at in range(hot_count):

        @pl.when(at < used)
        def _():
            entry = plan_ref[PLANE_LIST * hot_count + at]
            start_rows(plan_ref, entry, hot_count, adapter_device, local, arrived, copy_of(at))

    for at in range(hot_count):

        @pl.when(at < used)
        def _():
            copy_of(at)(local[0].at[0]).wait()

    share_rows(0, rank, hot_count, plan_ref, out_ref, shares)


def nothing_kernel(plan_ref, *outs):
    del plan_ref, outs


def hot_lanes(first_row, rows, hot_count, plan_ref):
    row_ids = first_row + lax.broadcasted_iota(jnp.int32, (1, rows), 1)
    hot = jnp.zeros((1, rows), jnp.int32)
    start = jnp.int32(0)
    for at in range(SECTIONS * hot_count + 3, plan_ref.shape[0], 2):
        end = plan_ref[at]
        hot = jnp.where((row_ids >= start) & (row_ids < end), plan_ref[at + 1], hot)
        start = end
    return hot


def partial_kernel(rank, hot_count, plan_ref, rows_ref, *refs):
    tokens = refs[:PLANE]
    outs = refs[PLANE:]
    device = lax.axis_index("seq")
    rows = tokens[0].shape[0]
    half = hot_count // 2

    def run(first, last):
        down = jnp.concatenate([rows_ref[at, :rank, :] for at in range(first, last)], axis=0).T
        for distance in range(PLANE):
            product = jnp.dot(
                tokens[distance][...], down, preferred_element_type=jnp.float32
            ).T
            hot = hot_lanes((device ^ distance) * rows, rows, hot_count, plan_ref)
            total = outs[distance][...] if first else jnp.zeros((rank, rows), jnp.float32)
            for at in range(first, last):
                piece = product[(at - first) * rank : (at - first + 1) * rank]
                total = jnp.where(hot == plan_ref[PLANE_LIST * hot_count + at], piece, total)
            outs[distance][...] = total

    run(0, half)

    @pl.when(plan_ref[SECTIONS * hot_count] > half)
    def _():
        run(half, hot_count)


def finish_kernel(
    hot_count,
    plan_ref,
    base_ref,
    cosine_ref,
    sine_ref,
    slot_ref,
    *refs,
):
    partials = refs[:PLANE]
    ups = refs[PLANE : 2 * PLANE]
    more = refs[2 * PLANE : 3 * PLANE]
    out_ref, low_ref, sum_ref, rows_ref = refs[3 * PLANE :]
    few, part, key_width = ups[0].shape
    rows = base_ref.shape[0]
    device = lax.axis_index("seq")
    place = lax.rem(device, PLANE)
    total = partials[0][...]
    for distance in range(1, PLANE):
        total = total + partials[distance][...]
    low_ref[...] = total
    hot = hot_lanes(device * rows, rows, hot_count, plan_ref)

    def adapted(held, first_entry):
        entries = []
        for at in range(first_entry, first_entry + held[0].shape[0]):
            listed = plan_ref[DEVICE_LISTS * hot_count + at]
            entry = plan_ref[PLANE_LIST * hot_count + jnp.maximum(listed, 0)]
            entries.append(jnp.where(listed >= 0, entry, -1))
        result = None
        for distance in range(PLANE):
            first = pl.multiple_of((place ^ distance) * part, part)
            piece = low_ref[pl.ds(first, part), :]
            spread_rows = jnp.concatenate(
                [jnp.where(hot == entry, piece, 0.0) for entry in entries], axis=0
            ).astype(jnp.bfloat16)
            product = lax.dot_general(
                spread_rows,
                held[distance][...].reshape(len(entries) * part, key_width),
                (((0,), (0,)), ((), ())),
                preferred_element_type=jnp.float32,
            )
            result = product if result is None else result + product
        return result

    sum_ref[...] = base_ref[...] + adapted(ups, 0)

    @pl.when(plan_ref[SECTIONS * hot_count + 2] == 0)
    def _():
        sum_ref[...] += adapted(more, few)

    projected = sum_ref[...]
    cosine = cosine_ref[...]
    sine = sine_ref[...]
    for head in range(key_width // HEAD):
        columns = slice(head * HEAD, (head + 1) * HEAD)
        values = projected[:, columns]
        turned = values * cosine + pltpu.roll(values, HEAD // 2, 1) * sine
        rows_ref[:, columns] = turned.astype(jnp.bfloat16)
    slots = lax.broadcasted_iota(jnp.int32, (out_ref.shape[0], rows), 0)
    placed = (slots == slot_ref[...]).astype(jnp.bfloat16)
    out_ref[...] = jnp.dot(
        placed, rows_ref[...], preferred_element_type=jnp.float32
    ).astype(jnp.bfloat16)


def turn_tables(positions):
    half_head = HEAD // 2
    frequencies = rope_theta ** (-(jnp.arange(half_head, dtype=jnp.float32) * 2.0) / HEAD)
    angles = positions.astype(jnp.float32)[:, None] * frequencies[None, :]
    cosine = jnp.cos(angles)
    sine = jnp.sin(angles)
    return (
        jnp.concatenate([cosine, cosine], axis=1),
        jnp.concatenate([-sine, sine], axis=1),
    )


def planes_outgoing(
    tokens,
    input_norm_scale,
    key_matrix,
    adapter_down_weight,
    adapter_up_weight,
    lengths,
    prompt_adapter_index,
    active_adapter_ids,
    positions,
    slot_index,
    out_rows,
):
    peer_count = PLANE * PLANES
    rows, width = tokens.shape
    quarter = width // PLANE
    adapter_device, rank, key_width = adapter_up_weight.shape
    part = rank // PLANE
    hot_count = active_adapter_ids.shape[0]
    prompt_index = prompt_adapter_index[:, 0]
    piece = jax.ShapeDtypeStruct((adapter_device, rank + part, quarter), jnp.bfloat16)
    packed = call(
        functools.partial(pack_kernel, quarter),
        [piece] * PLANE,
        [ANY, ANY],
        [ANY] * PLANE,
        [pltpu.SemaphoreType.DMA((2 * PLANE,))],
    )(jnp.swapaxes(adapter_down_weight, 1, 2), adapter_up_weight)
    packed = list(packed)
    local = [packed[0]] + [
        swap(packed[distance], distance, peer_count) for distance in range(1, PLANE)
    ]
    plan = call(
        functools.partial(plan_kernel, rows, adapter_device),
        jax.ShapeDtypeStruct((SECTIONS * hot_count + 3 + 2 * lengths.shape[0],), jnp.int32),
        [SMEM] * 3,
        SMEM,
    )(lengths, prompt_index, active_adapter_ids)
    tokens, packed[0] = lax.optimization_barrier((tokens, packed[0]))
    local[0] = packed[0]
    block = rows // 4
    normed, *columns = pl.pallas_call(
        norm_kernel,
        grid=(4,),
        out_shape=[jax.ShapeDtypeStruct((rows, width), jnp.bfloat16)]
        + [jax.ShapeDtypeStruct((rows, quarter), jnp.bfloat16)] * PLANE,
        in_specs=[
            pl.BlockSpec((block, width), lambda at: (at, 0)),
            pl.BlockSpec((1, width), lambda at: (0, 0)),
        ],
        out_specs=[pl.BlockSpec((block, width), lambda at: (at, 0))]
        + [pl.BlockSpec((block, quarter), lambda at: (at, 0))] * PLANE,
        compiler_params=pltpu.CompilerParams(vmem_limit_bytes=VMEM_LIMIT),
    )(tokens, input_norm_scale.reshape(1, width))
    base = jnp.dot(normed, key_matrix, preferred_element_type=jnp.float32)
    cosine, sine = turn_tables(positions)
    second = swap(columns[1], 1, peer_count)
    plan, base, cosine, sine, slot_index, second = lax.optimization_barrier(
        (plan, base, cosine, sine, slot_index, second)
    )

    def branch(slots):
        def run(plan, third, fourth, *local):
            sends = call(
                functools.partial(select_kernel, slots, hot_count, adapter_device),
                [
                    jax.ShapeDtypeStruct((slot, rank + part, quarter), jnp.bfloat16)
                    for slot in slots
                ],
                [SMEM] + [ANY] * PLANE,
                [ANY] * len(slots),
                [pltpu.SemaphoreType.DMA((sum(slots),))],
            )(plan, *local)
            *sends, third, fourth = lax.optimization_barrier((*sends, third, fourth))
            arrived = [
                swap(send, (at + 1) * PLANE, peer_count) for at, send in enumerate(sends)
            ]
            third = swap(third, 2, peer_count)
            fourth = swap(fourth, 3, peer_count)
            collected = call(
                functools.partial(collect_kernel, rank, hot_count, adapter_device),
                [jax.ShapeDtypeStruct((hot_count, rank + part, quarter), jnp.bfloat16)]
                + [jax.ShapeDtypeStruct((FEW, part, key_width), jnp.bfloat16)] * PLANE,
                [SMEM] + [ANY] * (PLANE + PLANES - 1),
                [VMEM] * (1 + PLANE),
                [pltpu.SemaphoreType.DMA((hot_count,))],
            )(plan, *local, *arrived)
            return (third, fourth, *collected)

        return run

    cases = [branch(slots) for slots in SLOT_CASES + ((hot_count,) * (PLANES - 1),)]
    third, fourth, used_rows, *ups = lax.switch(
        plan[SECTIONS * hot_count + 1], cases, plan, columns[2], columns[3], *local
    )

    def share(parts):
        return [parts[0]] + [
            swap(parts[distance], distance, peer_count) for distance in range(1, PLANE)
        ]

    def more_ups(plan, used_rows):
        return share(
            call(
                functools.partial(share_kernel, FEW, rank, hot_count),
                [jax.ShapeDtypeStruct((hot_count - FEW, part, key_width), jnp.bfloat16)] * PLANE,
                [SMEM, VMEM],
                [VMEM] * PLANE,
            )(plan, used_rows)
        )

    def no_more(plan, used_rows):
        del used_rows
        empty = call(
            nothing_kernel,
            [jax.ShapeDtypeStruct((hot_count - FEW, part, key_width), jnp.bfloat16)] * PLANE,
            [SMEM],
            [VMEM] * PLANE,
        )(plan)
        return list(empty)

    ups = share(ups)
    sums = call(
        functools.partial(partial_kernel, rank, hot_count),
        [jax.ShapeDtypeStruct((rank, rows), jnp.float32)] * PLANE,
        [SMEM] + [VMEM] * (1 + PLANE),
        [VMEM] * PLANE,
        flops=2 * hot_count * rank * width * rows,
        bytes_accessed=40 * 1024 * 1024,
    )(plan, used_rows, columns[0], second, third, fourth)
    partials = share(sums)
    late_plan, late_rows, _ = lax.optimization_barrier((plan, used_rows, sums[0]))
    more = lax.cond(
        late_plan[SECTIONS * hot_count + 2] == 1, no_more, more_ups, late_plan, late_rows
    )
    return call(
        functools.partial(finish_kernel, hot_count),
        jax.ShapeDtypeStruct((out_rows, key_width), jnp.bfloat16),
        [SMEM] + [VMEM] * (4 + 3 * PLANE),
        VMEM,
        [
            pltpu.VMEM((rank, rows), jnp.float32),
            pltpu.VMEM((rows, key_width), jnp.float32),
            pltpu.VMEM((rows, key_width), jnp.bfloat16),
        ],
        flops=2 * rows * key_width * (hot_count * rank + out_rows),
        bytes_accessed=6 * 1024 * 1024,
    )(
        plan,
        base,
        cosine,
        sine,
        slot_index.reshape(1, rows),
        *partials,
        *ups,
        *more,
    )


def gathered_outgoing(
    tokens,
    input_norm_scale,
    key_matrix,
    adapter_down_weight,
    adapter_up_weight,
    active_adapter_ids,
    positions,
    hot_slots,
    slot_index,
    out_rows,
):
    float_rows = tokens.astype(jnp.float32)
    inverse_rms = lax.rsqrt(jnp.mean(float_rows * float_rows, axis=1, keepdims=True) + norm_eps)
    normed = (float_rows * inverse_rms * input_norm_scale[None, :]).astype(jnp.bfloat16)
    adapter_device = adapter_down_weight.shape[0]
    down_list = []
    up_list = []
    for entry in range(active_adapter_ids.shape[0]):
        adapter = active_adapter_ids[entry]
        for weight, gathered in ((adapter_down_weight, down_list), (adapter_up_weight, up_list)):
            mine = lax.dynamic_index_in_dim(weight, adapter % adapter_device, 0, keepdims=False)
            gathered.append(spread(mine, "seq", adapter // adapter_device))
    down_matrices = jnp.concatenate(down_list, axis=1)
    up_matrices = jnp.concatenate(up_list, axis=0)
    base_proj = jnp.dot(normed, key_matrix, preferred_element_type=jnp.float32)
    low_rank = jnp.dot(normed, down_matrices, preferred_element_type=jnp.float32).astype(
        jnp.bfloat16
    )
    column_owned = (jnp.arange(down_matrices.shape[1], dtype=jnp.int32) // ADAPTER_RANK)[
        None, :
    ] == hot_slots[:, None]
    low_rank = jnp.where(column_owned, low_rank, jnp.zeros_like(low_rank))
    projected = base_proj + jnp.dot(low_rank, up_matrices, preferred_element_type=jnp.float32)
    key_rows = rotate(projected, positions).astype(jnp.bfloat16)
    return jnp.zeros((out_rows, key_rows.shape[1]), jnp.bfloat16).at[slot_index].set(key_rows)


def on_device(
    tokens,
    input_norm_scale,
    key_matrix,
    adapter_down_weight,
    adapter_up_weight,
    lengths,
    prompt_adapter_index,
    active_adapter_ids,
    token_cache_device,
):
    rows_dev = tokens.shape[0]
    peer_count = lax.axis_size("seq")
    slot_count = max(4, 2 * rows_dev // peer_count)
    key_width = key_matrix.shape[1]
    targets = token_cache_device[:, 0]
    row_order = jnp.arange(rows_dev, dtype=jnp.int32)
    earlier = row_order[None, :] < row_order[:, None]
    rank_within = jnp.sum(
        ((targets[:, None] == targets[None, :]) & earlier).astype(jnp.int32), axis=1
    )
    slot_index = targets * slot_count + rank_within
    positions, hot_slots = locate(
        lengths, prompt_adapter_index, lax.axis_index("seq") * rows_dev, rows_dev
    )
    out_rows = peer_count * slot_count
    if peer_count == PLANE * PLANES:
        outgoing = planes_outgoing(
            tokens,
            input_norm_scale,
            key_matrix,
            adapter_down_weight,
            adapter_up_weight,
            lengths,
            prompt_adapter_index,
            active_adapter_ids,
            positions,
            slot_index,
            out_rows,
        )
    else:
        outgoing = gathered_outgoing(
            tokens,
            input_norm_scale,
            key_matrix,
            adapter_down_weight,
            adapter_up_weight,
            active_adapter_ids,
            positions,
            hot_slots,
            slot_index,
            out_rows,
        )
    outgoing = outgoing.reshape(peer_count, slot_count, key_width)
    result = lax.all_to_all(outgoing, "seq", split_axis=0, concat_axis=0, tiled=True)
    return result.reshape(out_rows, key_width)


def solution(mesh):
    in_specs = (
        P(("groups", "seq"), None),
        P(),
        P(),
        P("seq", None, None),
        P("seq", None, None),
        P("groups"),
        P("groups", None),
        P("groups"),
        P(("groups", "seq"), None),
    )
    out_specs = P(("groups", "seq"), None)
    return jax.shard_map(
        on_device, mesh=mesh, in_specs=in_specs, out_specs=out_specs, check_vma=False
    )
```

profile of v0, /device:TPU:1, one launch (start us, length us, event | category | flops | bytes accessed | tf_op | source)
XLA Modules:
  0.0 106.3 jit_solution(15286092073139662266)
XLA Ops:
  0.0 1.2 %copy-done.1 = bf16[2,4096,64]{1,2,0:T(8,128)(2,1)S(1)} copy-done((bf16[2,4096,64]{1,2,0:T(8,128)(2,1)S(1)}, bf16[2,4096,64]{1,2,0:T(8,128)(2,1)}, u32[]{:S(2)}) %copy-start.1) | copy-done | bytes 1048600
  1.2 0.9 copy-done.2
  2.2 1.0 shard_map.92
  3.2 0.0 copy-start.4
  3.2 0.0 copy-start.10
  3.3 0.0 copy-start
  3.3 1.6 %copy-done = bf16[256,4096]{1,0:T(8,128)(2,1)S(1)} copy-done((bf16[256,4096]{1,0:T(8,128)(2,1)S(1)}, bf16[256,4096]{1,0:T(8,128)(2,1)}, u32[]{:S(2)}) %copy-start) | copy-done | bytes 2097176
  4.8 2.4 %shard_map.93 = (bf16[256,4096]{1,0:T(8,128)(2,1)S(1)}, bf16[256,1024]{1,0:T(8,128)(2,1)S(1)}, bf16[256,1024]{1,0:T(8,128)(2,1)}, bf16[256,1024]{1,0:T(8,128)(2,1)}, bf16[256,1024]{1,0:T(8,128)(2,1)}) custom-call(bf16[256,4096]{1,0:T(8,128)(2,1)S(1)} %copy-done, f32[1,4096]{1,0:T(1,128)S(1)} %bitcast.16), custom_call_target="tpu_custom_call" | custom-call | tf_op jit(solution)/shard_map/pallas_call | solution.py:479
  7.3 0.8 copy-done.7
  8.0 0.1 collective-permute-start.43
  8.1 0.5 collective-permute-start.44
  8.6 2.2 %collective-permute-start.45 = (bf16[2,80,1024]{2,1,0:T(8,128)(2,1)}, bf16[2,80,1024]{2,1,0:T(8,128)(2,1)}, u32[]{:S(2)}, u32[]{:S(2)}) collective-permute-start(bf16[2,80,1024]{2,1,0:T(8,128)(2,1)} %get-tuple-element.333), channel_id=1, source_target_pairs={{0,2},{1,3},{2,0},{3,1},{4,6},{5,7},{6,4},{7,5},{8,10},{9,11},{10,... | collective-permute-start | bytes 983048 | tf_op jit(solution)/shard_map/ppermute | solution.py:64
  10.8 0.4 collective-permute-start.46
  11.2 0.2 reduce-window.8
  11.4 0.1 convert_reduce_fusion.1
  11.5 0.1 select_reduce_fusion
  11.6 0.2 convert_reduce_fusion
  11.8 0.0 copy-start.6
  11.8 5.9 %fusion.2.base_ref = f32[256,1024]{1,0:T(8,128)S(1)} fusion(bf16[256,4096]{1,0:T(8,128)(2,1)S(1)} %get-tuple-element.324, bf16[4096,1024]{1,0:T(8,128)(2,1)} %param.21), kind=kOutput, calls=%fused_computation.16 | convolution fusion | flops 2147483648 | bytes 11534336 | tf_op jit(solution)/shard_map/dot_general | solution.py:492
  17.7 2.0 %shard_map.91.plan_ref = s32[99]{0:T(128)S(1)} custom-call(s32[8]{0:T(128)S(1)} %copy-done.4, s32[8]{0:T(128)S(1)} %bitcast.19, s32[8]{0:T(128)S(1)} %copy-done.6), custom_call_target="tpu_custom_call" | custom-call | tf_op jit(solution)/shard_map/pallas_call | solution.py:470
  19.7 0.5 fusion.1
  20.2 0.1 pad_maximum_fusion
  20.4 0.6 slice.6
  21.6 4.4 %collective-permute-done.46 = bf16[2,80,1024]{2,1,0:T(8,128)(2,1)} collective-permute-done((bf16[2,80,1024]{2,1,0:T(8,128)(2,1)S(1)}, bf16[2,80,1024]{2,1,0:T(8,128)(2,1)}, u32[]{:S(2)}, u32[]{:S(2)}) %collective-permute-start.46) | collective-permute-done | bytes 327712 | tf_op jit(solution)/shard_map/ppermute | solution.py:64
  26.1 29.0 %conditional.2 = (bf16[256,1024]{1,0:T(8,128)(2,1)}, bf16[256,1024]{1,0:T(8,128)(2,1)}, bf16[8,80,1024]{2,1,0:T(8,128)(2,1)S(1)}, bf16[4,16,1024]{2,1,0:T(8,128)...) conditional(s32[]{:T(128)} %bitcast.7, (s32[99]{0:T(128)S(1)}, ...), branch_computations={%region_4.5_spmd, %region_5.6_spmd, %region_6.7_spmd, %region_7.8_... | conditional | bytes 19923200 | solution.py:530
  26.1 2.0 %branch_2_fun.2 = (bf16[3,80,1024]{2,1,0:T(8,128)(2,1)S(1)}, bf16[1,80,1024]{2,1,0:T(8,128)(2,1)S(1)}, bf16[2,80,1024]{2,1,0:T(8,128)(2,1)S(1)}) custom-call(s32[99]{0:T(128)S(1)} %get-tuple-element.162.plan_ref, bf16[2,80,1024]{2,1,0:T(8,128)(2,1)S(1)} %get-tuple-element.163.refs_0_, bf16[2,80,1024]{2,1,0:T(8,128)(2,1)} %get-tuple-element.164.refs_1_, ...), custom_call_target="tpu_custom_call" | custom-call | tf_op jit(solution)/shard_map/cond/branch_2_fun/pallas_call | solution.py:501
  28.1 1.4 %collective-permute-start.10 = (bf16[256,1024]{1,0:T(8,128)(2,1)S(1)}, bf16[256,1024]{1,0:T(8,128)(2,1)}, u32[]{:S(2)}, u32[]{:S(2)}) collective-permute-start(bf16[256,1024]{1,0:T(8,128)(2,1)S(1)} %get-tuple-element.172), channel_id=1, source_target_pairs={{0,2},{1,3},{2,0},{3,1},{4,6},{5,7},{6,4},{7,5},{8,10},{9,11},{10,... | collective-permute-start | bytes 1572872 | tf_op jit(solution)/shard_map/cond/branch_2_fun/ppermute | solution.py:64
  29.6 0.5 collective-permute-start.11
  30.1 1.1 %collective-permute-start.12 = (bf16[3,80,1024]{2,1,0:T(8,128)(2,1)S(1)}, bf16[3,80,1024]{2,1,0:T(8,128)(2,1)S(1)}, u32[]{:S(2)}, u32[]{:S(2)}) collective-permute-start(bf16[3,80,1024]{2,1,0:T(8,128)(2,1)S(1)} %get-tuple-element.174), channel_id=1, source_target_pairs={{0,4},{1,5},{2,6},{3,7},{4,0},{5,1},{6,2},{7,3},{8,12},{9,13},{10,... | collective-permute-start | bytes 1474568 | tf_op jit(solution)/shard_map/cond/branch_2_fun/ppermute | solution.py:64
  31.2 2.3 %collective-permute-start.14 = (bf16[2,80,1024]{2,1,0:T(8,128)(2,1)S(1)}, bf16[2,80,1024]{2,1,0:T(8,128)(2,1)S(1)}, u32[]{:S(2)}, u32[]{:S(2)}) collective-permute-start(bf16[2,80,1024]{2,1,0:T(8,128)(2,1)S(1)} %get-tuple-element.176), channel_id=1, source_target_pairs={{0,12},{1,13},{2,14},{3,15},{4,8},{5,9},{6,10},{7,11},{8,4},{9,5},... | collective-permute-start | bytes 983048 | tf_op jit(solution)/shard_map/cond/branch_2_fun/ppermute | solution.py:64
  33.5 18.5 %collective-permute-done.13.refs_5_ = bf16[1,80,1024]{2,1,0:T(8,128)(2,1)S(1)} collective-permute-done((bf16[1,80,1024]{2,1,0:T(8,128)(2,1)S(1)}, bf16[1,80,1024]{2,1,0:T(8,128)(2,1)S(1)}, u32[]{:S(2)}, u32[]{:S(2)}) %collective-permute-start.13) | collective-permute-done | bytes 163872 | tf_op jit(solution)/shard_map/cond/branch_2_fun/ppermute | solution.py:64
  52.0 1.5 %collective-permute-done.12.refs_4_ = bf16[3,80,1024]{2,1,0:T(8,128)(2,1)S(1)} collective-permute-done((bf16[3,80,1024]{2,1,0:T(8,128)(2,1)S(1)}, bf16[3,80,1024]{2,1,0:T(8,128)(2,1)S(1)}, u32[]{:S(2)}, u32[]{:S(2)}) %collective-permute-start.12) | collective-permute-done | bytes 491552 | tf_op jit(solution)/shard_map/cond/branch_2_fun/ppermute | solution.py:64
  53.5 1.4 %branch_2_fun.3 = (bf16[8,80,1024]{2,1,0:T(8,128)(2,1)S(1)}, bf16[4,16,1024]{2,1,0:T(8,128)(2,1)S(1)}, bf16[4,16,1024]{2,1,0:T(8,128)(2,1)S(1)}, bf16[4,16,1024]...) custom-call(s32[99]{0:T(128)S(1)} %get-tuple-element.162.plan_ref, bf16[2,80,1024]{2,1,0:T(8,128)(2,1)S(1)} %get-tuple-element.163.refs_0_, ...), custom_call_target="tpu_custom_call" | custom-call | tf_op jit(solution)/shard_map/cond/branch_2_fun/pallas_call | solution.py:517
  55.2 2.3 %shard_map.94 = (f32[64,256]{1,0:T(8,128)S(1)}, f32[64,256]{1,0:T(8,128)S(1)}, f32[64,256]{1,0:T(8,128)S(1)}, f32[64,256]{1,0:T(8,128)S(1)}) custom-call(s32[99]{0:T(128)S(1)} %shard_map.91.plan_ref, bf16[8,80,1024]{2,1,0:T(8,128)(2,1)S(1)} %get-tuple-element.351.rows_ref, bf16[256,1024]{1,0:T(8,128)(2,1)S(1)} %copy-done.8, ...), custom_call_target="tpu_custom_call" | custom-call | flops 1073741824 | bytes 41943040 | tf_op jit(solution)/shard_map/pallas_call | solution.py:560
  57.4 0.6 slice.7
  58.7 0.8 collective-permute-start.47
  59.5 0.1 collective-permute-start.50
  59.6 0.5 conditional.3
  59.6 0.5 branch_1_fun.5
  60.1 0.9 collective-permute-start.51
  61.0 1.2 %collective-permute-start.52 = (bf16[4,16,1024]{2,1,0:T(8,128)(2,1)S(1)}, bf16[4,16,1024]{2,1,0:T(8,128)(2,1)S(1)}, u32[]{:S(2)}, u32[]{:S(2)}) collective-permute-start(bf16[4,16,1024]{2,1,0:T(8,128)(2,1)S(1)} %get-tuple-element.349), channel_id=1, source_target_pairs={{0,3},{1,2},{2,1},{3,0},{4,7},{5,6},{6,5},{7,4},{8,11},{9,10},{10,... | collective-permute-start | bytes 393224 | tf_op jit(solution)/shard_map/ppermute | solution.py:64
  62.2 0.8 collective-permute-start.48
  63.1 0.6 collective-permute-start.49
  63.7 5.1 %collective-permute-done.48.refs_2_ = f32[64,256]{1,0:T(8,128)S(1)} collective-permute-done((f32[64,256]{1,0:T(8,128)S(1)}, f32[64,256]{1,0:T(8,128)S(1)}, u32[]{:S(2)}, u32[]{:S(2)}) %collective-permute-start.48) | collective-permute-done | bytes 65568 | tf_op jit(solution)/shard_map/ppermute | solution.py:64
  68.7 2.3 %collective-permute-done.49.refs_3_ = f32[64,256]{1,0:T(8,128)S(1)} collective-permute-done((f32[64,256]{1,0:T(8,128)S(1)}, f32[64,256]{1,0:T(8,128)S(1)}, u32[]{:S(2)}, u32[]{:S(2)}) %collective-permute-start.49) | collective-permute-done | bytes 65568 | tf_op jit(solution)/shard_map/ppermute | solution.py:64
  71.0 2.0 %shard_map.95 = bf16[512,1024]{1,0:T(8,128)(2,1)S(1)} custom-call(s32[99]{0:T(128)S(1)} %shard_map.91.plan_ref, f32[256,1024]{1,0:T(8,128)S(1)} %fusion.2.base_ref, f32[256,128]{1,0:T(8,128)S(1)} %get-tuple-element.328.cosine_ref, f32[256,128]{1,0:T(8,128)S(1)} %get-tuple-element.329.sine_ref, s32[1,256]{1,0:T(1,128)S(1)} %bitcast.17, ...), custom_call_target="tpu_custom_call" | custom-call | flops 536870912 | bytes 6291456 | tf_op jit(solution)/shard_map/pallas_call | solution.py:573
  73.0 32.3 %all_to_all.5 = bf16[16,32,1024]{2,1,0:T(8,128)(2,1)S(1)} all-to-all(bf16[16,32,1024]{2,1,0:T(8,128)(2,1)S(1)} %bitcast.14), channel_id=1, replica_groups=mesh['groups'=2,'seq'=16] {'seq'}, dimensions={0} | all-to-all | bytes 2097152 | tf_op jit(solution)/shard_map/all_to_all | solution.py:689
  105.3 1.0 copy.75
  (34 shorter events, 0.1 us)
Async XLA Ops:
  0.0 1.2 %copy-start.1 = (bf16[2,4096,64]{1,2,0:T(8,128)(2,1)S(1)}, bf16[2,4096,64]{1,2,0:T(8,128)(2,1)}, u32[]{:S(2)}) copy-start(bf16[2,4096,64]{1,2,0:T(8,128)(2,1)} %param.22) | copy-start | bytes 3145732
  1.2 0.9 copy-start.2
  2.2 1.1 %copy-start.3 = (f32[4096]{0:T(1024)S(1)}, f32[4096]{0:T(1024)}, u32[]{:S(2)}) copy-start(f32[4096]{0:T(1024)} %param.20) | copy-start | bytes 49156
  3.2 8.0 %copy-start.4 = (s32[8]{0:T(128)S(1)}, s32[8]{0:T(128)}, u32[]{:S(2)}) copy-start(s32[8]{0:T(128)} %length_ref.1) | copy-start | bytes 100
  3.2 8.4 %copy-start.10 = (s32[256,1]{0,1:T(1,128)S(1)}, s32[256,1]{0,1:T(1,128)}, u32[]{:S(2)}) copy-start(s32[256,1]{0,1:T(1,128)} %param.27) | copy-start | bytes 3076
  3.3 1.6 %copy-start = (bf16[256,4096]{1,0:T(8,128)(2,1)S(1)}, bf16[256,4096]{1,0:T(8,128)(2,1)}, u32[]{:S(2)}) copy-start(bf16[256,4096]{1,0:T(8,128)(2,1)} %token_ref) | copy-start | bytes 6291460
  7.3 0.8 copy-start.7
  8.0 12.3 %collective-permute-start.43 = (bf16[256,1024]{1,0:T(8,128)(2,1)}, bf16[256,1024]{1,0:T(8,128)(2,1)}, u32[]{:S(2)}, u32[]{:S(2)}) collective-permute-start(bf16[256,1024]{1,0:T(8,128)(2,1)} %get-tuple-element.325), channel_id=1, source_target_pairs={{0,1},{1,0},{2,3},{3,2},{4,5},{5,4},{6,7},{7,6},{8,9},{9,8},{10,11... | collective-permute-start | bytes 1572872 | tf_op jit(solution)/shard_map/ppermute | solution.py:64
  8.1 13.5 %collective-permute-start.44 = (bf16[2,80,1024]{2,1,0:T(8,128)(2,1)}, bf16[2,80,1024]{2,1,0:T(8,128)(2,1)}, u32[]{:S(2)}, u32[]{:S(2)}) collective-permute-start(bf16[2,80,1024]{2,1,0:T(8,128)(2,1)} %get-tuple-element.332), channel_id=1, source_target_pairs={{0,1},{1,0},{2,3},{3,2},{4,5},{5,4},{6,7},{7,6},{8,9},{9,8},{10,11... | collective-permute-start | bytes 983048 | tf_op jit(solution)/shard_map/ppermute | solution.py:64
  8.6 13.1 %collective-permute-start.45 = (bf16[2,80,1024]{2,1,0:T(8,128)(2,1)}, bf16[2,80,1024]{2,1,0:T(8,128)(2,1)}, u32[]{:S(2)}, u32[]{:S(2)}) collective-permute-start(bf16[2,80,1024]{2,1,0:T(8,128)(2,1)} %get-tuple-element.333), channel_id=1, source_target_pairs={{0,2},{1,3},{2,0},{3,1},{4,6},{5,7},{6,4},{7,5},{8,10},{9,11},{10,... | collective-permute-start | bytes 983048 | tf_op jit(solution)/shard_map/ppermute | solution.py:64
  10.8 15.3 %collective-permute-start.46 = (bf16[2,80,1024]{2,1,0:T(8,128)(2,1)S(1)}, bf16[2,80,1024]{2,1,0:T(8,128)(2,1)}, u32[]{:S(2)}, u32[]{:S(2)}) collective-permute-start(bf16[2,80,1024]{2,1,0:T(8,128)(2,1)S(1)} %get-tuple-element.334), channel_id=1, source_target_pairs={{0,3},{1,2},{2,1},{3,0},{4,7},{5,6},{6,5},{7,4},{8,11},{9,10},{10,... | collective-permute-start | bytes 983048 | tf_op jit(solution)/shard_map/ppermute | solution.py:64
  11.8 5.9 %copy-start.5 = (s32[8,1]{0,1:T(1,128)S(1)}, s32[8,1]{0,1:T(1,128)}, u32[]{:S(2)}) copy-start(s32[8,1]{0,1:T(1,128)} %param.25) | copy-start | bytes 100
  11.8 5.9 %copy-start.6 = (s32[8]{0:T(128)S(1)}, s32[8]{0:T(128)}, u32[]{:S(2)}) copy-start(s32[8]{0:T(128)} %id_ref.1) | copy-start | bytes 100
  11.8 14.3 %copy-start.9 = (bf16[2,80,1024]{2,1,0:T(8,128)(2,1)S(1)}, bf16[2,80,1024]{2,1,0:T(8,128)(2,1)}, u32[]{:S(2)}) copy-start(bf16[2,80,1024]{2,1,0:T(8,128)(2,1)} %get-tuple-element.331) | copy-start | bytes 983044
  11.8 14.3 %copy-start.11 = (bf16[256,1024]{1,0:T(8,128)(2,1)S(1)}, bf16[256,1024]{1,0:T(8,128)(2,1)}, u32[]{:S(2)}) copy-start(bf16[256,1024]{1,0:T(8,128)(2,1)} %get-tuple-element.335) | copy-start | bytes 1572868
  11.8 14.3 %copy-start.12 = (bf16[256,1024]{1,0:T(8,128)(2,1)S(1)}, bf16[256,1024]{1,0:T(8,128)(2,1)}, u32[]{:S(2)}) copy-start(bf16[256,1024]{1,0:T(8,128)(2,1)} %get-tuple-element.336) | copy-start | bytes 1572868
  26.1 29.1 %copy-start.8 = (bf16[256,1024]{1,0:T(8,128)(2,1)S(1)}, bf16[256,1024]{1,0:T(8,128)(2,1)}, u32[]{:S(2)}) copy-start(bf16[256,1024]{1,0:T(8,128)(2,1)} %copy-done.7) | copy-start | bytes 1572868
  28.1 26.8 %collective-permute-start.10 = (bf16[256,1024]{1,0:T(8,128)(2,1)S(1)}, bf16[256,1024]{1,0:T(8,128)(2,1)}, u32[]{:S(2)}, u32[]{:S(2)}) collective-permute-start(bf16[256,1024]{1,0:T(8,128)(2,1)S(1)} %get-tuple-element.172), channel_id=1, source_target_pairs={{0,2},{1,3},{2,0},{3,1},{4,6},{5,7},{6,4},{7,5},{8,10},{9,11},{10,... | collective-permute-start | bytes 1572872 | tf_op jit(solution)/shard_map/cond/branch_2_fun/ppermute | solution.py:64
  29.6 25.4 %collective-permute-start.11 = (bf16[256,1024]{1,0:T(8,128)(2,1)S(1)}, bf16[256,1024]{1,0:T(8,128)(2,1)}, u32[]{:S(2)}, u32[]{:S(2)}) collective-permute-start(bf16[256,1024]{1,0:T(8,128)(2,1)S(1)} %get-tuple-element.173), channel_id=1, source_target_pairs={{0,3},{1,2},{2,1},{3,0},{4,7},{5,6},{6,5},{7,4},{8,11},{9,10},{10,... | collective-permute-start | bytes 1572872 | tf_op jit(solution)/shard_map/cond/branch_2_fun/ppermute | solution.py:64
  30.1 23.4 %collective-permute-start.12 = (bf16[3,80,1024]{2,1,0:T(8,128)(2,1)S(1)}, bf16[3,80,1024]{2,1,0:T(8,128)(2,1)S(1)}, u32[]{:S(2)}, u32[]{:S(2)}) collective-permute-start(bf16[3,80,1024]{2,1,0:T(8,128)(2,1)S(1)} %get-tuple-element.174), channel_id=1, source_target_pairs={{0,4},{1,5},{2,6},{3,7},{4,0},{5,1},{6,2},{7,3},{8,12},{9,13},{10,... | collective-permute-start | bytes 1474568 | tf_op jit(solution)/shard_map/cond/branch_2_fun/ppermute | solution.py:64
  31.2 20.8 %collective-permute-start.14 = (bf16[2,80,1024]{2,1,0:T(8,128)(2,1)S(1)}, bf16[2,80,1024]{2,1,0:T(8,128)(2,1)S(1)}, u32[]{:S(2)}, u32[]{:S(2)}) collective-permute-start(bf16[2,80,1024]{2,1,0:T(8,128)(2,1)S(1)} %get-tuple-element.176), channel_id=1, source_target_pairs={{0,12},{1,13},{2,14},{3,15},{4,8},{5,9},{6,10},{7,11},{8,4},{9,5},... | collective-permute-start | bytes 983048 | tf_op jit(solution)/shard_map/cond/branch_2_fun/ppermute | solution.py:64
  33.5 18.5 %collective-permute-start.13 = (bf16[1,80,1024]{2,1,0:T(8,128)(2,1)S(1)}, bf16[1,80,1024]{2,1,0:T(8,128)(2,1)S(1)}, u32[]{:S(2)}, u32[]{:S(2)}) collective-permute-start(bf16[1,80,1024]{2,1,0:T(8,128)(2,1)S(1)} %get-tuple-element.175), channel_id=1, source_target_pairs={{0,8},{1,9},{2,10},{3,11},{4,12},{5,13},{6,14},{7,15},{8,0},{9,1},... | collective-permute-start | bytes 491528 | tf_op jit(solution)/shard_map/cond/branch_2_fun/ppermute | solution.py:64
  58.7 4.4 %collective-permute-start.47 = (f32[64,256]{1,0:T(8,128)S(1)}, f32[64,256]{1,0:T(8,128)S(1)}, u32[]{:S(2)}, u32[]{:S(2)}) collective-permute-start(f32[64,256]{1,0:T(8,128)S(1)} %get-tuple-element.343), channel_id=1, source_target_pairs={{0,1},{1,0},{2,3},{3,2},{4,5},{5,4},{6,7},{7,6},{8,9},{9,8},{10,11... | collective-permute-start | bytes 196616 | tf_op jit(solution)/shard_map/ppermute | solution.py:64
  59.5 11.5 %collective-permute-start.50 = (bf16[4,16,1024]{2,1,0:T(8,128)(2,1)S(1)}, bf16[4,16,1024]{2,1,0:T(8,128)(2,1)S(1)}, u32[]{:S(2)}, u32[]{:S(2)}) collective-permute-start(bf16[4,16,1024]{2,1,0:T(8,128)(2,1)S(1)} %get-tuple-element.347), channel_id=1, source_target_pairs={{0,1},{1,0},{2,3},{3,2},{4,5},{5,4},{6,7},{7,6},{8,9},{9,8},{10,11... | collective-permute-start | bytes 393224 | tf_op jit(solution)/shard_map/ppermute | solution.py:64
  60.1 10.9 %collective-permute-start.51 = (bf16[4,16,1024]{2,1,0:T(8,128)(2,1)S(1)}, bf16[4,16,1024]{2,1,0:T(8,128)(2,1)S(1)}, u32[]{:S(2)}, u32[]{:S(2)}) collective-permute-start(bf16[4,16,1024]{2,1,0:T(8,128)(2,1)S(1)} %get-tuple-element.348), channel_id=1, source_target_pairs={{0,2},{1,3},{2,0},{3,1},{4,6},{5,7},{6,4},{7,5},{8,10},{9,11},{10,... | collective-permute-start | bytes 393224 | tf_op jit(solution)/shard_map/ppermute | solution.py:64
  61.0 10.0 %collective-permute-start.52 = (bf16[4,16,1024]{2,1,0:T(8,128)(2,1)S(1)}, bf16[4,16,1024]{2,1,0:T(8,128)(2,1)S(1)}, u32[]{:S(2)}, u32[]{:S(2)}) collective-permute-start(bf16[4,16,1024]{2,1,0:T(8,128)(2,1)S(1)} %get-tuple-element.349), channel_id=1, source_target_pairs={{0,3},{1,2},{2,1},{3,0},{4,7},{5,6},{6,5},{7,4},{8,11},{9,10},{10,... | collective-permute-start | bytes 393224 | tf_op jit(solution)/shard_map/ppermute | solution.py:64
  62.2 6.5 %collective-permute-start.48 = (f32[64,256]{1,0:T(8,128)S(1)}, f32[64,256]{1,0:T(8,128)S(1)}, u32[]{:S(2)}, u32[]{:S(2)}) collective-permute-start(f32[64,256]{1,0:T(8,128)S(1)} %get-tuple-element.344), channel_id=1, source_target_pairs={{0,2},{1,3},{2,0},{3,1},{4,6},{5,7},{6,4},{7,5},{8,10},{9,11},{10,... | collective-permute-start | bytes 196616 | tf_op jit(solution)/shard_map/ppermute | solution.py:64
  63.1 7.9 %collective-permute-start.49 = (f32[64,256]{1,0:T(8,128)S(1)}, f32[64,256]{1,0:T(8,128)S(1)}, u32[]{:S(2)}, u32[]{:S(2)}) collective-permute-start(f32[64,256]{1,0:T(8,128)S(1)} %get-tuple-element.345), channel_id=1, source_target_pairs={{0,3},{1,2},{2,1},{3,0},{4,7},{5,6},{6,5},{7,4},{8,11},{9,10},{10,... | collective-permute-start | bytes 196616 | tf_op jit(solution)/shard_map/ppermute | solution.py:64
where the time goes:
time: 105 us; the launch traced here: 106 us
  blocking collectives  32.3 us (31%)
  waiting for transfers between devices  31.8 us (30%)
  Pallas kernels  13.6 us (13%)
  starting transfers between devices  13 us (12%)
  local copies, waits for them, and re-layouts  6.73 us (6%)
  matrix products  5.87 us (6%)
  between operations  1.54 us (1%)
  other arithmetic  1.23 us (1%)
    all_to_all x1, blocking collectives, on_device(): lax.all_to_all(outgoing, 'seq', split_axis=0, concat_axis=0, tiled=True)  32.3 us
    ppermute x15, waiting for transfers between devices, swap(): lax.ppermute(value, 'seq', [(i, i ^ distance) for i in range(peer_count)])  31.8 us
    ppermute x15, starting transfers between devices, swap(): lax.ppermute(value, 'seq', [(i, i ^ distance) for i in range(peer_count)])  13 us
    dot_general x1, matrix products, planes_outgoing(): base = jnp.dot(normed, key_matrix, preferred_element_type=jnp.float32)  5.87 us
    unnamed x27, local copies, waits for them, and re-layouts  5.56 us
    pallas_call x1, Pallas kernels, planes_outgoing(): pl.pallas_call(norm_kernel, grid=(4,), out_shape=[jax.ShapeDtypeStruct((r...  2.4 us
    pallas_call x1, Pallas kernels, planes_outgoing(): call(functools.partial(partial_kernel, rank, hot_count), [jax.ShapeDtypeS...  2.26 us
  transfers between devices with their start and end apart: 15, of which 5 were waited for; matrix products, arithmetic and copies ran while one was open for 7% of the time, Pallas kernels for 4%

commit v1 on v0

--- a/solution.py
+++ b/solution.py
@@ -53,7 +53,7 @@
 PLANE = 4
 PLANES = 4
 SLOT_CASES = ((2, 1, 1), (3, 2, 1), (3, 1, 2), (3, 2, 2), (3, 3, 1), (3, 1, 3), (4, 3, 3))
-FEW = 4
+FEW = 3
 ANY = pl.BlockSpec(memory_space=pl.ANY)
 SMEM = pl.BlockSpec(memory_space=pltpu.SMEM)
 VMEM = pl.BlockSpec(memory_space=pltpu.VMEM)
@@ -185,7 +185,7 @@
         few = few & (count <= FEW)
     case = jnp.int32(len(SLOT_CASES))
     for at in reversed(range(len(SLOT_CASES))):
-        fits = jnp.bool_(True)
+        fits = few
         for distance in range(PLANES - 1):
             fits = fits & (most[distance] <= SLOT_CASES[at][distance])
         case = jnp.where(fits, at, case)
@@ -279,21 +279,21 @@
             copy_of(arrived[distance - 1].at[slot]).start()
 
 
-def share_rows(first, rank, hot_count, plan_ref, rows_ref, outs):
+def share_rows(first, count, rank, hot_count, plan_ref, rows_ref, outs):
     for distance in range(PLANE):
-        for at in range(outs[0].shape[0]):
+        for at in range(count):
             listed = plan_ref[(DEVICE_LISTS + distance) * hot_count + first + at]
             outs[distance][at] = rows_ref[jnp.maximum(listed, 0), rank:, :]
 
 
 def share_kernel(first, rank, hot_count, plan_ref, rows_ref, *outs):
-    share_rows(first, rank, hot_count, plan_ref, rows_ref, outs)
-
-
-def collect_kernel(rank, hot_count, adapter_device, plan_ref, *refs):
+    share_rows(first, outs[0].shape[0], rank, hot_count, plan_ref, rows_ref, outs)
+
+
+def collect_kernel(hot_count, adapter_device, plan_ref, *refs):
     local = refs[:PLANE]
     arrived = refs[PLANE : PLANE + PLANES - 1]
-    out_ref, *shares, sems = refs[PLANE + PLANES - 1 :]
+    out_ref, sems = refs[PLANE + PLANES - 1], refs[-1]
     used = plan_ref[SECTIONS * hot_count]
 
     def copy_of(at):
@@ -311,12 +311,6 @@
         @pl.when(at < used)
         def _():
             copy_of(at)(local[0].at[0]).wait()
-
-    share_rows(0, rank, hot_count, plan_ref, out_ref, shares)
-
-
-def nothing_kernel(plan_ref, *outs):
-    del plan_ref, outs
 
 
 def hot_lanes(first_row, rows, hot_count, plan_ref):
@@ -332,10 +326,13 @@
 
 def partial_kernel(rank, hot_count, plan_ref, rows_ref, *refs):
     tokens = refs[:PLANE]
-    outs = refs[PLANE:]
+    outs = refs[PLANE : 2 * PLANE]
+    sums = refs[2 * PLANE]
     device = lax.axis_index("seq")
     rows = tokens[0].shape[0]
     half = hot_count // 2
+    part = rank // PLANE
+    share_rows(0, FEW, rank, hot_count, plan_ref, rows_ref, outs)
 
     def run(first, last):
         down = jnp.concatenate([rows_ref[at, :rank, :] for at in range(first, last)], axis=0).T
@@ -344,17 +341,25 @@
                 tokens[distance][...], down, preferred_element_type=jnp.float32
             ).T
             hot = hot_lanes((device ^ distance) * rows, rows, hot_count, plan_ref)
-            total = outs[distance][...] if first else jnp.zeros((rank, rows), jnp.float32)
+            total = sums[distance] if first else jnp.zeros((rank, rows), jnp.float32)
             for at in range(first, last):
                 piece = product[(at - first) * rank : (at - first + 1) * rank]
                 total = jnp.where(hot == plan_ref[PLANE_LIST * hot_count + at], piece, total)
-            outs[distance][...] = total
+            sums[distance] = total
 
     run(0, half)
 
     @pl.when(plan_ref[SECTIONS * hot_count] > half)
     def _():
         run(half, hot_count)
+
+    for distance in range(PLANE):
+        for at in range(PLANE):
+            total = sums[distance, at * part : (at + 1) * part]
+            high = total.astype(jnp.bfloat16)
+            low = (total - high.astype(jnp.float32)).astype(jnp.bfloat16)
+            outs[distance][FEW, :, at * rows : (at + 1) * rows] = high
+            outs[distance][FEW + 1, :, at * rows : (at + 1) * rows] = low
 
 
 def finish_kernel(
@@ -366,23 +371,26 @@
     slot_ref,
     *refs,
 ):
-    partials = refs[:PLANE]
-    ups = refs[PLANE : 2 * PLANE]
-    more = refs[2 * PLANE : 3 * PLANE]
-    out_ref, low_ref, sum_ref, rows_ref = refs[3 * PLANE :]
-    few, part, key_width = ups[0].shape
+    shared = refs[:PLANE]
+    more = refs[PLANE : 2 * PLANE]
+    out_ref, low_ref, sum_ref, rows_ref = refs[2 * PLANE :]
+    _, part, key_width = shared[0].shape
     rows = base_ref.shape[0]
     device = lax.axis_index("seq")
     place = lax.rem(device, PLANE)
-    total = partials[0][...]
-    for distance in range(1, PLANE):
-        total = total + partials[distance][...]
-    low_ref[...] = total
+    for at in range(PLANE):
+        total = jnp.zeros((part, rows), jnp.float32)
+        for distance in range(PLANE):
+            for term in (FEW, FEW + 1):
+                total = total + shared[distance][term, :, at * rows : (at + 1) * rows].astype(
+                    jnp.float32
+                )
+        low_ref[at * part : (at + 1) * part] = total
     hot = hot_lanes(device * rows, rows, hot_count, plan_ref)
 
-    def adapted(held, first_entry):
+    def adapted(held, first_entry, count):
         entries = []
-        for at in range(first_entry, first_entry + held[0].shape[0]):
+        for at in range(first_entry, first_entry + count):
             listed = plan_ref[DEVICE_LISTS * hot_count + at]
             entry = plan_ref[PLANE_LIST * hot_count + jnp.maximum(listed, 0)]
             entries.append(jnp.where(listed >= 0, entry, -1))
@@ -395,18 +403,18 @@
             ).astype(jnp.bfloat16)
             product = lax.dot_general(
                 spread_rows,
-                held[distance][...].reshape(len(entries) * part, key_width),
+                held[distance][:count].reshape(count * part, key_width),
                 (((0,), (0,)), ((), ())),
                 preferred_element_type=jnp.float32,
             )
             result = product if result is None else result + product
         return result
 
-    sum_ref[...] = base_ref[...] + adapted(ups, 0)
+    sum_ref[...] = base_ref[...] + adapted(shared, 0, FEW)
 
     @pl.when(plan_ref[SECTIONS * hot_count + 2] == 0)
     def _():
-        sum_ref[...] += adapted(more, few)
+        sum_ref[...] += adapted(more, FEW, hot_count - FEW)
 
     projected = sum_ref[...]
     cosine = cosine_ref[...]
@@ -463,7 +471,6 @@
         [ANY] * PLANE,
         [pltpu.SemaphoreType.DMA((2 * PLANE,))],
     )(jnp.swapaxes(adapter_down_weight, 1, 2), adapter_up_weight)
-    packed = list(packed)
     local = [packed[0]] + [
         swap(packed[distance], distance, peer_count) for distance in range(1, PLANE)
     ]
@@ -473,8 +480,7 @@
         [SMEM] * 3,
         SMEM,
     )(lengths, prompt_index, active_adapter_ids)
-    tokens, packed[0] = lax.optimization_barrier((tokens, packed[0]))
-    local[0] = packed[0]
+    tokens, local[1] = lax.optimization_barrier((tokens, local[1]))
     block = rows // 4
     normed, *columns = pl.pallas_call(
         norm_kernel,
@@ -496,6 +502,13 @@
         (plan, base, cosine, sine, slot_index, second)
     )
 
+    rest = jax.ShapeDtypeStruct((hot_count - FEW, part, key_width), jnp.bfloat16)
+
+    def share(parts):
+        return [parts[0]] + [
+            swap(parts[distance], distance, peer_count) for distance in range(1, PLANE)
+        ]
+
     def branch(slots):
         def run(plan, third, fourth, *local):
             sends = call(
@@ -514,66 +527,47 @@
             ]
             third = swap(third, 2, peer_count)
             fourth = swap(fourth, 3, peer_count)
-            collected = call(
-                functools.partial(collect_kernel, rank, hot_count, adapter_device),
+            collected, *more = call(
+                functools.partial(collect_kernel, hot_count, adapter_device),
                 [jax.ShapeDtypeStruct((hot_count, rank + part, quarter), jnp.bfloat16)]
-                + [jax.ShapeDtypeStruct((FEW, part, key_width), jnp.bfloat16)] * PLANE,
+                + ([] if slots[0] == hot_count else [rest] * PLANE),
                 [SMEM] + [ANY] * (PLANE + PLANES - 1),
-                [VMEM] * (1 + PLANE),
+                [VMEM] * (1 if slots[0] == hot_count else 1 + PLANE),
                 [pltpu.SemaphoreType.DMA((hot_count,))],
             )(plan, *local, *arrived)
-            return (third, fourth, *collected)
+            if not more:
+                more = share(
+                    call(
+                        functools.partial(share_kernel, FEW, rank, hot_count),
+                        [rest] * PLANE,
+                        [SMEM, VMEM],
+                        [VMEM] * PLANE,
+                    )(plan, collected)
+                )
+            return (third, fourth, collected, *more)
 
         return run
 
     cases = [branch(slots) for slots in SLOT_CASES + ((hot_count,) * (PLANES - 1),)]
-    third, fourth, used_rows, *ups = lax.switch(
+    third, fourth, used_rows, *more = lax.switch(
         plan[SECTIONS * hot_count + 1], cases, plan, columns[2], columns[3], *local
     )
 
-    def share(parts):
-        return [parts[0]] + [
-            swap(parts[distance], distance, peer_count) for distance in range(1, PLANE)
-        ]
-
-    def more_ups(plan, used_rows):
-        return share(
-            call(
-                functools.partial(share_kernel, FEW, rank, hot_count),
-                [jax.ShapeDtypeStruct((hot_count - FEW, part, key_width), jnp.bfloat16)] * PLANE,
-                [SMEM, VMEM],
-                [VMEM] * PLANE,
-            )(plan, used_rows)
-        )
-
-    def no_more(plan, used_rows):
-        del used_rows
-        empty = call(
-            nothing_kernel,
-            [jax.ShapeDtypeStruct((hot_count - FEW, part, key_width), jnp.bfloat16)] * PLANE,
-            [SMEM],
+    shared = share(
+        call(
+            functools.partial(partial_kernel, rank, hot_count),
+            [jax.ShapeDtypeStruct((FEW + 2, part, key_width), jnp.bfloat16)] * PLANE,
+            [SMEM] + [VMEM] * (1 + PLANE),
             [VMEM] * PLANE,
-        )(plan)
-        return list(empty)
-
-    ups = share(ups)
-    sums = call(
-        functools.partial(partial_kernel, rank, hot_count),
-        [jax.ShapeDtypeStruct((rank, rows), jnp.float32)] * PLANE,
-        [SMEM] + [VMEM] * (1 + PLANE),
-        [VMEM] * PLANE,
-        flops=2 * hot_count * rank * width * rows,
-        bytes_accessed=40 * 1024 * 1024,
-    )(plan, used_rows, columns[0], second, third, fourth)
-    partials = share(sums)
-    late_plan, late_rows, _ = lax.optimization_barrier((plan, used_rows, sums[0]))
-    more = lax.cond(
-        late_plan[SECTIONS * hot_count + 2] == 1, no_more, more_ups, late_plan, late_rows
+            [pltpu.VMEM((PLANE, rank, rows), jnp.float32)],
+            flops=2 * hot_count * rank * width * rows,
+            bytes_accessed=6 * 1024 * 1024,
+        )(plan, used_rows, columns[0], second, third, fourth)
     )
     return call(
         functools.partial(finish_kernel, hot_count),
         jax.ShapeDtypeStruct((out_rows, key_width), jnp.bfloat16),
-        [SMEM] + [VMEM] * (4 + 3 * PLANE),
+        [SMEM] + [VMEM] * (4 + 2 * PLANE),
         VMEM,
         [
             pltpu.VMEM((rank, rows), jnp.float32),
@@ -588,8 +582,7 @@
         cosine,
         sine,
         slot_index.reshape(1, rows),
-        *partials,
-        *ups,
+        *shared,
         *more,
     )
 

time: 105 us -> 97.7 us (0.930); the launches traced: 106 us -> 97.7 us
  waiting for transfers between devices: 31.8 us -> 24.2 us
  other arithmetic: 1.23 us -> 3.97 us
  starting transfers between devices: 13 us -> 11.5 us
  blocking collectives: 32.3 us -> 31 us
    ppermute x15 -> x12, waiting for transfers between devices: 31.8 us -> 24.2 us  [swap(): lax.ppermute(value, 'seq', [(i, i ^ distance) for i in range(peer_count)])]
    ppermute x15 -> x12, starting transfers between devices: 13 us -> 11.5 us  [swap(): lax.ppermute(value, 'seq', [(i, i ^ distance) for i in range(peer_count)])]
    all_to_all x1, blocking collectives: 32.3 us -> 31 us  [on_device(): lax.all_to_all(outgoing, 'seq', split_axis=0, concat_axis=0, tiled=True)]
    pallas_call x1, Pallas kernels: 2.4 us -> 1.27 us  [planes_outgoing(): pl.pallas_call(norm_kernel, grid=(4,), out_shape=[jax.ShapeDtypeStruct((r...]
    pallas_call x2 -> x1, Pallas kernels: 1.94 us -> 2.82 us  [run(): call(functools.partial(collect_kernel, hot_count, adapter_device), [jax.S...]
    unnamed x27 -> x21, local copies, waits for them, and re-layouts: 5.56 us -> 6.01 us
  transfers between devices with their start and end apart: 15 -> 12, of which waited for: 5 -> 5; matrix products, arithmetic and copies ran while one was open for 7% -> 11% of each run, Pallas kernels for 4% -> 6%
where the time goes in v1:
time: 97.7 us
  blocking collectives  31 us (32%)
  waiting for transfers between devices  24.2 us (25%)
  Pallas kernels  13.8 us (14%)
  starting transfers between devices  11.5 us (12%)
  local copies, waits for them, and re-layouts  6.6 us (7%)
  matrix products  5.77 us (6%)
  other arithmetic  3.97 us (4%)
    all_to_all x1, blocking collectives, on_device(): lax.all_to_all(outgoing, 'seq', split_axis=0, concat_axis=0, tiled=True)  31 us
    ppermute x12, waiting for transfers between devices, swap(): lax.ppermute(value, 'seq', [(i, i ^ distance) for i in range(peer_count)])  24.2 us
    ppermute x12, starting transfers between devices, swap(): lax.ppermute(value, 'seq', [(i, i ^ distance) for i in range(peer_count)])  11.5 us
    unnamed x21, local copies, waits for them, and re-layouts  6.01 us
    dot_general x1, matrix products, planes_outgoing(): base = jnp.dot(normed, key_matrix, preferred_element_type=jnp.float32)  5.77 us
    pallas_call x1, Pallas kernels, run(): call(functools.partial(collect_kernel, hot_count, adapter_device), [jax.S...  2.82 us
    pallas_call x1, Pallas kernels, planes_outgoing(): call(functools.partial(finish_kernel, hot_count), jax.ShapeDtypeStruct((o...  2.56 us
    pallas_call x1, Pallas kernels, planes_outgoing(): call(functools.partial(partial_kernel, rank, hot_count), [jax.ShapeDtypeS...  2.52 us
  transfers between devices with their start and end apart: 12, of which 5 were waited for; matrix products, arithmetic and copies ran while one was open for 11% of the time, Pallas kernels for 6%

profile of v1, /device:TPU:1, one launch (start us, length us, event | category | flops | bytes accessed | tf_op | source)
XLA Modules:
  0.0 97.7 jit_solution(15499340060492469921)
XLA Ops:
  0.0 1.4 %copy-done.1 = bf16[2,4096,64]{1,2,0:T(8,128)(2,1)S(1)} copy-done((bf16[2,4096,64]{1,2,0:T(8,128)(2,1)S(1)}, bf16[2,4096,64]{1,2,0:T(8,128)(2,1)}, u32[]{:S(2)}) %copy-start.1) | copy-done | bytes 1048600
  1.4 0.9 copy-done.2
  2.3 1.0 %shard_map.92 = (bf16[2,80,1024]{2,1,0:T(8,128)(2,1)}, bf16[2,80,1024]{2,1,0:T(8,128)(2,1)S(1)}, bf16[2,80,1024]{2,1,0:T(8,128)(2,1)}, bf16[2,80,1024]{2,1,0:T(8,128)(2,1)}) custom-call(bf16[2,64,4096]{2,1,0:T(8,128)(2,1)S(1)} %bitcast.14, bf16[2,64,1024]{2,1,0:T(8,128)(2,1)S(1)} %copy-done.2), custom_call_target="tpu_custom_call" | custom-call | tf_op jit(solution)/shard_map/pallas_call | solution.py:467
  3.3 0.1 collective-permute-start.43
  3.5 2.7 %collective-permute-start.45 = (bf16[2,80,1024]{2,1,0:T(8,128)(2,1)}, bf16[2,80,1024]{2,1,0:T(8,128)(2,1)}, u32[]{:S(2)}, u32[]{:S(2)}) collective-permute-start(bf16[2,80,1024]{2,1,0:T(8,128)(2,1)} %get-tuple-element.315), channel_id=1, source_target_pairs={{0,2},{1,3},{2,0},{3,1},{4,6},{5,7},{6,4},{7,5},{8,10},{9,11},{10,... | collective-permute-start | bytes 983048 | tf_op jit(solution)/shard_map/ppermute | solution.py:64
  6.1 0.0 collective-permute-start.46
  6.2 0.8 reduce-window.8
  7.0 0.7 bitcast_subtract_fusion
  7.7 0.1 convert_reduce_fusion.1
  7.8 0.1 select_reduce_fusion
  7.9 0.9 convert_reduce_fusion
  8.8 0.5 fusion.1
  9.3 0.0 copy-start.4
  9.4 0.6 copy-done.4
  10.0 0.7 copy-done.5
  10.7 0.7 copy-done.6
  11.3 2.0 %shard_map.91.plan_ref = s32[99]{0:T(128)S(1)} custom-call(s32[8]{0:T(128)S(1)} %copy-done.4, s32[8]{0:T(128)S(1)} %bitcast.18, s32[8]{0:T(128)S(1)} %copy-done.6), custom_call_target="tpu_custom_call" | custom-call | tf_op jit(solution)/shard_map/pallas_call | solution.py:477
  13.3 0.1 pad_maximum_fusion
  13.4 0.7 multiply_add_fusion
  14.1 0.0 collective-permute-done.43
  14.1 0.7 copy-done.8
  14.9 1.3 %shard_map.93 = (bf16[256,4096]{1,0:T(8,128)(2,1)S(1)}, bf16[256,1024]{1,0:T(8,128)(2,1)S(1)}, bf16[256,1024]{1,0:T(8,128)(2,1)S(1)}, bf16[256,1024]{1,0:T(8,128)(2,1)S(1)}, bf16[256,1024]{1,0:T(8,128)(2,1)S(1)}) custom-call(bf16[256,4096]{1,0:T(8,128)(2,1)S(1)} %copy-done, f32[1,4096]{1,0:T(1,128)S(1)} %bitcast.15), custom_call_target="tpu_custom_call" | custom-call | tf_op jit(solution)/shard_map/pallas_call | solution.py:485
  16.1 0.4 collective-permute-start.44
  16.6 5.8 %fusion.2.base_ref = f32[256,1024]{1,0:T(8,128)S(1)} fusion(bf16[256,4096]{1,0:T(8,128)(2,1)S(1)} %get-tuple-element.306, bf16[4096,1024]{1,0:T(8,128)(2,1)} %param.19), kind=kOutput, calls=%fused_computation.16 | convolution fusion | flops 2147483648 | bytes 11534336 | tf_op jit(solution)/shard_map/dot_general | solution.py:498
  22.3 0.0 collective-permute-done.44.refs_1_
  22.4 0.6 slice.3
  23.6 27.3 %conditional.1 = (bf16[256,1024]{1,0:T(8,128)(2,1)}, bf16[256,1024]{1,0:T(8,128)(2,1)}, bf16[8,80,1024]{2,1,0:T(8,128)(2,1)}, bf16[5,16,1024]{2,1,0:T(8,128)(2,1...) conditional(s32[]{:T(128)} %bitcast.7, (s32[99]{0:T(128)S(1)}, ...), branch_computations={%region_4.5_spmd, %region_5.6_spmd, %region_6.7_spmd, %region_7.8_... | conditional | bytes 21889400 | solution.py:552
  23.6 1.7 %branch_0_fun.2 = (bf16[2,80,1024]{2,1,0:T(8,128)(2,1)S(1)}, bf16[1,80,1024]{2,1,0:T(8,128)(2,1)S(1)}, bf16[1,80,1024]{2,1,0:T(8,128)(2,1)S(1)}) custom-call(s32[99]{0:T(128)S(1)} %get-tuple-element.117.plan_ref, bf16[2,80,1024]{2,1,0:T(8,128)(2,1)S(1)} %get-tuple-element.118.refs_0_, bf16[2,80,1024]{2,1,0:T(8,128)(2,1)S(1)} %get-tuple-element.119.refs_1_, ...), custom_call_target="tpu_custom_call" | custom-call | tf_op jit(solution)/shard_map/cond/branch_0_fun/pallas_call | solution.py:514
  25.3 2.0 %collective-permute-start = (bf16[256,1024]{1,0:T(8,128)(2,1)S(1)}, bf16[256,1024]{1,0:T(8,128)(2,1)}, u32[]{:S(2)}, u32[]{:S(2)}) collective-permute-start(bf16[256,1024]{1,0:T(8,128)(2,1)S(1)} %get-tuple-element.127), channel_id=1, source_target_pairs={{0,2},{1,3},{2,0},{3,1},{4,6},{5,7},{6,4},{7,5},{8,10},{9,11},{10,... | collective-permute-start | bytes 1572872 | tf_op jit(solution)/shard_map/cond/branch_0_fun/ppermute | solution.py:64
  27.4 0.3 collective-permute-start.1
  27.7 1.4 %collective-permute-start.2 = (bf16[2,80,1024]{2,1,0:T(8,128)(2,1)S(1)}, bf16[2,80,1024]{2,1,0:T(8,128)(2,1)S(1)}, u32[]{:S(2)}, u32[]{:S(2)}) collective-permute-start(bf16[2,80,1024]{2,1,0:T(8,128)(2,1)S(1)} %get-tuple-element.129), channel_id=1, source_target_pairs={{0,4},{1,5},{2,6},{3,7},{4,0},{5,1},{6,2},{7,3},{8,12},{9,13},{10,... | collective-permute-start | bytes 983048 | tf_op jit(solution)/shard_map/cond/branch_0_fun/ppermute | solution.py:64
  29.1 2.2 %collective-permute-start.3 = (bf16[1,80,1024]{2,1,0:T(8,128)(2,1)S(1)}, bf16[1,80,1024]{2,1,0:T(8,128)(2,1)S(1)}, u32[]{:S(2)}, u32[]{:S(2)}) collective-permute-start(bf16[1,80,1024]{2,1,0:T(8,128)(2,1)S(1)} %get-tuple-element.130), channel_id=1, source_target_pairs={{0,8},{1,9},{2,10},{3,11},{4,12},{5,13},{6,14},{7,15},{8,0},{9,1},... | collective-permute-start | bytes 491528 | tf_op jit(solution)/shard_map/cond/branch_0_fun/ppermute | solution.py:64
  31.3 0.1 collective-permute-start.4
  31.3 8.6 %collective-permute-done.3.refs_5_ = bf16[1,80,1024]{2,1,0:T(8,128)(2,1)S(1)} collective-permute-done((bf16[1,80,1024]{2,1,0:T(8,128)(2,1)S(1)}, bf16[1,80,1024]{2,1,0:T(8,128)(2,1)S(1)}, u32[]{:S(2)}, u32[]{:S(2)}) %collective-permute-start.3) | collective-permute-done | bytes 163872 | tf_op jit(solution)/shard_map/cond/branch_0_fun/ppermute | solution.py:64
  39.9 6.5 %collective-permute-done.4.refs_6_ = bf16[1,80,1024]{2,1,0:T(8,128)(2,1)S(1)} collective-permute-done((bf16[1,80,1024]{2,1,0:T(8,128)(2,1)S(1)}, bf16[1,80,1024]{2,1,0:T(8,128)(2,1)S(1)}, u32[]{:S(2)}, u32[]{:S(2)}) %collective-permute-start.4) | collective-permute-done | bytes 163872 | tf_op jit(solution)/shard_map/cond/branch_0_fun/ppermute | solution.py:64
  46.4 0.0 collective-permute-done.2.refs_4_
  46.4 2.8 %branch_0_fun.3 = (bf16[8,80,1024]{2,1,0:T(8,128)(2,1)}, bf16[5,16,1024]{2,1,0:T(8,128)(2,1)S(1)}, bf16[5,16,1024]{2,1,0:T(8,128)(2,1)}, bf16[5,16,1024]{2,1,0:T(8,128)(2,1)}, bf16[5,16,1024]{2,1,0:T(8,128)(2,1)}) custom-call(s32[99]{0:T(128)S(1)} %get-tuple-element.117.plan_ref, bf16[2,80,1024]{2,1,0:T(8,128)(2,1)S(1)} %get-tuple-element.118.refs_0_, ...), custom_call_target="tpu_custom_call" | custom-call | tf_op jit(solution)/shard_map/cond/branch_0_fun/pallas_call | solution.py:530
  49.2 1.6 %collective-permute-done.1 = bf16[256,1024]{1,0:T(8,128)(2,1)} collective-permute-done((bf16[256,1024]{1,0:T(8,128)(2,1)S(1)}, bf16[256,1024]{1,0:T(8,128)(2,1)}, u32[]{:S(2)}, u32[]{:S(2)}) %collective-permute-start.1) | collective-permute-done | bytes 524320 | tf_op jit(solution)/shard_map/cond/branch_0_fun/ppermute | solution.py:64
  50.9 2.5 %shard_map.94 = (bf16[5,16,1024]{2,1,0:T(8,128)(2,1)S(1)}, bf16[5,16,1024]{2,1,0:T(8,128)(2,1)S(1)}, bf16[5,16,1024]{2,1,0:T(8,128)(2,1)S(1)}, bf16[5,16,1024]{2,1,0:T(8,128)(2,1)S(1)}) custom-call(s32[99]{0:T(128)S(1)} %shard_map.91.plan_ref, bf16[8,80,1024]{2,1,0:T(8,128)(2,1)} %get-tuple-element.319.rows_ref, ...), custom_call_target="tpu_custom_call" | custom-call | flops 1073741824 | bytes 6291456 | tf_op jit(solution)/shard_map/pallas_call | solution.py:557
  53.4 0.3 collective-permute-start.47
  53.7 1.3 %collective-permute-start.48 = (bf16[5,16,1024]{2,1,0:T(8,128)(2,1)S(1)}, bf16[5,16,1024]{2,1,0:T(8,128)(2,1)S(1)}, u32[]{:S(2)}, u32[]{:S(2)}) collective-permute-start(bf16[5,16,1024]{2,1,0:T(8,128)(2,1)S(1)} %get-tuple-element.326), channel_id=1, source_target_pairs={{0,2},{1,3},{2,0},{3,1},{4,6},{5,7},{6,4},{7,5},{8,10},{9,11},{10,... | collective-permute-start | bytes 491528 | tf_op jit(solution)/shard_map/ppermute | solution.py:64
  55.0 0.6 collective-permute-start.49
  55.6 0.0 collective-permute-done.47.refs_1_
  55.6 3.6 %collective-permute-done.48.refs_2_ = bf16[5,16,1024]{2,1,0:T(8,128)(2,1)S(1)} collective-permute-done((bf16[5,16,1024]{2,1,0:T(8,128)(2,1)S(1)}, bf16[5,16,1024]{2,1,0:T(8,128)(2,1)S(1)}, u32[]{:S(2)}, u32[]{:S(2)}) %collective-permute-start.48) | collective-permute-done | bytes 163872 | tf_op jit(solution)/shard_map/ppermute | solution.py:64
  59.2 3.9 %collective-permute-done.49.refs_3_ = bf16[5,16,1024]{2,1,0:T(8,128)(2,1)S(1)} collective-permute-done((bf16[5,16,1024]{2,1,0:T(8,128)(2,1)S(1)}, bf16[5,16,1024]{2,1,0:T(8,128)(2,1)S(1)}, u32[]{:S(2)}, u32[]{:S(2)}) %collective-permute-start.49) | collective-permute-done | bytes 163872 | tf_op jit(solution)/shard_map/ppermute | solution.py:64
  63.1 2.6 %shard_map.95 = bf16[512,1024]{1,0:T(8,128)(2,1)S(1)} custom-call(s32[99]{0:T(128)S(1)} %shard_map.91.plan_ref, f32[256,1024]{1,0:T(8,128)S(1)} %fusion.2.base_ref, f32[256,128]{1,0:T(8,128)S(1)} %get-tuple-element.310.cosine_ref, f32[256,128]{1,0:T(8,128)S(1)} %get-tuple-element.311.sine_ref, s32[1,256]{1,0:T(1,128)S(1)} %bitcast.16, ...), custom_call_target="tpu_custom_call" | custom-call | flops 536870912 | bytes 6291456 | tf_op jit(solution)/shard_map/pallas_call | solution.py:567
  65.7 31.0 %all_to_all.5 = bf16[16,32,1024]{2,1,0:T(8,128)(2,1)S(1)} all-to-all(bf16[16,32,1024]{2,1,0:T(8,128)(2,1)S(1)} %bitcast.13), channel_id=1, replica_groups=mesh['groups'=2,'seq'=16] {'seq'}, dimensions={0} | all-to-all | bytes 2097152 | tf_op jit(solution)/shard_map/all_to_all | solution.py:682
  96.7 1.0 copy.67
  (19 shorter events, 0.1 us)
Async XLA Ops:
  0.0 14.9 %copy-start = (bf16[256,4096]{1,0:T(8,128)(2,1)S(1)}, bf16[256,4096]{1,0:T(8,128)(2,1)}, u32[]{:S(2)}) copy-start(bf16[256,4096]{1,0:T(8,128)(2,1)} %token_ref) | copy-start | bytes 6291460
  0.0 1.4 %copy-start.1 = (bf16[2,4096,64]{1,2,0:T(8,128)(2,1)S(1)}, bf16[2,4096,64]{1,2,0:T(8,128)(2,1)}, u32[]{:S(2)}) copy-start(bf16[2,4096,64]{1,2,0:T(8,128)(2,1)} %param.20) | copy-start | bytes 3145732
  1.4 0.9 copy-start.2
  2.3 12.5 %copy-start.3 = (f32[4096]{0:T(1024)S(1)}, f32[4096]{0:T(1024)}, u32[]{:S(2)}) copy-start(f32[4096]{0:T(1024)} %param.18) | copy-start | bytes 49156
  3.3 10.8 %collective-permute-start.43 = (bf16[2,80,1024]{2,1,0:T(8,128)(2,1)S(1)}, bf16[2,80,1024]{2,1,0:T(8,128)(2,1)S(1)}, u32[]{:S(2)}, u32[]{:S(2)}) collective-permute-start(bf16[2,80,1024]{2,1,0:T(8,128)(2,1)S(1)} %get-tuple-element.304), channel_id=1, source_target_pairs={{0,1},{1,0},{2,3},{3,2},{4,5},{5,4},{6,7},{7,6},{8,9},{9,8},{10,11... | collective-permute-start | bytes 983048 | tf_op jit(solution)/shard_map/ppermute | solution.py:64
  3.5 20.1 %collective-permute-start.45 = (bf16[2,80,1024]{2,1,0:T(8,128)(2,1)}, bf16[2,80,1024]{2,1,0:T(8,128)(2,1)}, u32[]{:S(2)}, u32[]{:S(2)}) collective-permute-start(bf16[2,80,1024]{2,1,0:T(8,128)(2,1)} %get-tuple-element.315), channel_id=1, source_target_pairs={{0,2},{1,3},{2,0},{3,1},{4,6},{5,7},{6,4},{7,5},{8,10},{9,11},{10,... | collective-permute-start | bytes 983048 | tf_op jit(solution)/shard_map/ppermute | solution.py:64
  6.1 17.5 %collective-permute-start.46 = (bf16[2,80,1024]{2,1,0:T(8,128)(2,1)}, bf16[2,80,1024]{2,1,0:T(8,128)(2,1)}, u32[]{:S(2)}, u32[]{:S(2)}) collective-permute-start(bf16[2,80,1024]{2,1,0:T(8,128)(2,1)} %get-tuple-element.316), channel_id=1, source_target_pairs={{0,3},{1,2},{2,1},{3,0},{4,7},{5,6},{6,5},{7,4},{8,11},{9,10},{10,... | collective-permute-start | bytes 983048 | tf_op jit(solution)/shard_map/ppermute | solution.py:64
  9.3 0.7 copy-start.4
  10.0 0.7 copy-start.5
  10.7 0.7 copy-start.6
  14.1 0.7 copy-start.8
  16.1 6.2 %collective-permute-start.44 = (bf16[256,1024]{1,0:T(8,128)(2,1)S(1)}, bf16[256,1024]{1,0:T(8,128)(2,1)S(1)}, u32[]{:S(2)}, u32[]{:S(2)}) collective-permute-start(bf16[256,1024]{1,0:T(8,128)(2,1)S(1)} %get-tuple-element.307), channel_id=1, source_target_pairs={{0,1},{1,0},{2,3},{3,2},{4,5},{5,4},{6,7},{7,6},{8,9},{9,8},{10,11... | collective-permute-start | bytes 1572872 | tf_op jit(solution)/shard_map/ppermute | solution.py:64
  16.6 7.0 %copy-start.7 = (bf16[2,80,1024]{2,1,0:T(8,128)(2,1)S(1)}, bf16[2,80,1024]{2,1,0:T(8,128)(2,1)}, u32[]{:S(2)}) copy-start(bf16[2,80,1024]{2,1,0:T(8,128)(2,1)} %get-tuple-element.313) | copy-start | bytes 983044
  16.6 7.0 %copy-start.9 = (bf16[2,80,1024]{2,1,0:T(8,128)(2,1)S(1)}, bf16[2,80,1024]{2,1,0:T(8,128)(2,1)}, u32[]{:S(2)}) copy-start(bf16[2,80,1024]{2,1,0:T(8,128)(2,1)} %copy-done.8) | copy-start | bytes 983044
  25.3 23.9 %collective-permute-start = (bf16[256,1024]{1,0:T(8,128)(2,1)S(1)}, bf16[256,1024]{1,0:T(8,128)(2,1)}, u32[]{:S(2)}, u32[]{:S(2)}) collective-permute-start(bf16[256,1024]{1,0:T(8,128)(2,1)S(1)} %get-tuple-element.127), channel_id=1, source_target_pairs={{0,2},{1,3},{2,0},{3,1},{4,6},{5,7},{6,4},{7,5},{8,10},{9,11},{10,... | collective-permute-start | bytes 1572872 | tf_op jit(solution)/shard_map/cond/branch_0_fun/ppermute | solution.py:64
  27.4 23.5 %collective-permute-start.1 = (bf16[256,1024]{1,0:T(8,128)(2,1)S(1)}, bf16[256,1024]{1,0:T(8,128)(2,1)}, u32[]{:S(2)}, u32[]{:S(2)}) collective-permute-start(bf16[256,1024]{1,0:T(8,128)(2,1)S(1)} %get-tuple-element.128), channel_id=1, source_target_pairs={{0,3},{1,2},{2,1},{3,0},{4,7},{5,6},{6,5},{7,4},{8,11},{9,10},{10,... | collective-permute-start | bytes 1572872 | tf_op jit(solution)/shard_map/cond/branch_0_fun/ppermute | solution.py:64
  27.7 18.7 %collective-permute-start.2 = (bf16[2,80,1024]{2,1,0:T(8,128)(2,1)S(1)}, bf16[2,80,1024]{2,1,0:T(8,128)(2,1)S(1)}, u32[]{:S(2)}, u32[]{:S(2)}) collective-permute-start(bf16[2,80,1024]{2,1,0:T(8,128)(2,1)S(1)} %get-tuple-element.129), channel_id=1, source_target_pairs={{0,4},{1,5},{2,6},{3,7},{4,0},{5,1},{6,2},{7,3},{8,12},{9,13},{10,... | collective-permute-start | bytes 983048 | tf_op jit(solution)/shard_map/cond/branch_0_fun/ppermute | solution.py:64
  29.1 10.8 %collective-permute-start.3 = (bf16[1,80,1024]{2,1,0:T(8,128)(2,1)S(1)}, bf16[1,80,1024]{2,1,0:T(8,128)(2,1)S(1)}, u32[]{:S(2)}, u32[]{:S(2)}) collective-permute-start(bf16[1,80,1024]{2,1,0:T(8,128)(2,1)S(1)} %get-tuple-element.130), channel_id=1, source_target_pairs={{0,8},{1,9},{2,10},{3,11},{4,12},{5,13},{6,14},{7,15},{8,0},{9,1},... | collective-permute-start | bytes 491528 | tf_op jit(solution)/shard_map/cond/branch_0_fun/ppermute | solution.py:64
  31.3 15.1 %collective-permute-start.4 = (bf16[1,80,1024]{2,1,0:T(8,128)(2,1)S(1)}, bf16[1,80,1024]{2,1,0:T(8,128)(2,1)S(1)}, u32[]{:S(2)}, u32[]{:S(2)}) collective-permute-start(bf16[1,80,1024]{2,1,0:T(8,128)(2,1)S(1)} %get-tuple-element.131), channel_id=1, source_target_pairs={{0,12},{1,13},{2,14},{3,15},{4,8},{5,9},{6,10},{7,11},{8,4},{9,5},... | collective-permute-start | bytes 491528 | tf_op jit(solution)/shard_map/cond/branch_0_fun/ppermute | solution.py:64
  53.4 2.2 %collective-permute-start.47 = (bf16[5,16,1024]{2,1,0:T(8,128)(2,1)S(1)}, bf16[5,16,1024]{2,1,0:T(8,128)(2,1)S(1)}, u32[]{:S(2)}, u32[]{:S(2)}) collective-permute-start(bf16[5,16,1024]{2,1,0:T(8,128)(2,1)S(1)} %get-tuple-element.325), channel_id=1, source_target_pairs={{0,1},{1,0},{2,3},{3,2},{4,5},{5,4},{6,7},{7,6},{8,9},{9,8},{10,11... | collective-permute-start | bytes 491528 | tf_op jit(solution)/shard_map/ppermute | solution.py:64
  53.7 5.5 %collective-permute-start.48 = (bf16[5,16,1024]{2,1,0:T(8,128)(2,1)S(1)}, bf16[5,16,1024]{2,1,0:T(8,128)(2,1)S(1)}, u32[]{:S(2)}, u32[]{:S(2)}) collective-permute-start(bf16[5,16,1024]{2,1,0:T(8,128)(2,1)S(1)} %get-tuple-element.326), channel_id=1, source_target_pairs={{0,2},{1,3},{2,0},{3,1},{4,6},{5,7},{6,4},{7,5},{8,10},{9,11},{10,... | collective-permute-start | bytes 491528 | tf_op jit(solution)/shard_map/ppermute | solution.py:64
  55.0 8.1 %collective-permute-start.49 = (bf16[5,16,1024]{2,1,0:T(8,128)(2,1)S(1)}, bf16[5,16,1024]{2,1,0:T(8,128)(2,1)S(1)}, u32[]{:S(2)}, u32[]{:S(2)}) collective-permute-start(bf16[5,16,1024]{2,1,0:T(8,128)(2,1)S(1)} %get-tuple-element.327), channel_id=1, source_target_pairs={{0,3},{1,2},{2,1},{3,0},{4,7},{5,6},{6,5},{7,4},{8,11},{9,10},{10,... | collective-permute-start | bytes 491528 | tf_op jit(solution)/shard_map/ppermute | solution.py:64

commit v2 on v1

--- a/solution.py
+++ b/solution.py
@@ -52,7 +52,19 @@
 
 PLANE = 4
 PLANES = 4
-SLOT_CASES = ((2, 1, 1), (3, 2, 1), (3, 1, 2), (3, 2, 2), (3, 3, 1), (3, 1, 3), (4, 3, 3))
+SLOT_CASES = (
+    (2, 1, 1),
+    (3, 2, 1),
+    (3, 1, 2),
+    (3, 2, 2),
+    (3, 3, 1),
+    (3, 1, 3),
+    (4, 3, 2),
+    (4, 2, 3),
+    (4, 4, 1),
+    (4, 1, 4),
+    (4, 3, 3),
+)
 FEW = 3
 ANY = pl.BlockSpec(memory_space=pl.ANY)
 SMEM = pl.BlockSpec(memory_space=pltpu.SMEM)
@@ -237,46 +249,17 @@
 
 def select_kernel(slots, hot_count, adapter_device, plan_ref, *refs):
     local = refs[:PLANE]
-    outs = refs[PLANE : PLANE + PLANES - 1]
-    sems = refs[-1]
-    waits = []
+    outs = refs[PLANE:]
     for distance in range(1, PLANES):
         for slot in range(slots[distance - 1]):
             index = plan_ref[(distance - 1) * hot_count + slot]
             holder = lax.div(index, adapter_device)
             inner = index - holder * adapter_device
-            target = outs[distance - 1].at[slot]
-            sem = sems.at[len(waits)]
             for at in range(PLANE):
 
                 @pl.when(holder == at)
                 def _():
-                    pltpu.make_async_copy(local[at].at[inner], target, sem).start()
-
-            waits.append(pltpu.make_async_copy(local[0].at[0], target, sem))
-    for wait in waits:
-        wait.wait()
-
-
-def start_rows(plan_ref, entry, hot_count, adapter_device, local, arrived, copy_of):
-    kind = plan_ref[FROM_KIND * hot_count + entry]
-    slot = plan_ref[FROM_SLOT * hot_count + entry]
-
-    @pl.when(kind == 0)
-    def _():
-        holder = lax.div(slot, adapter_device)
-        inner = slot - holder * adapter_device
-        for at in range(PLANE):
-
-            @pl.when(holder == at)
-            def _():
-                copy_of(local[at].at[inner]).start()
-
-    for distance in range(1, PLANES):
-
-        @pl.when(kind == distance)
-        def _():
-            copy_of(arrived[distance - 1].at[slot]).start()
+                    outs[distance - 1][slot] = local[at][inner]
 
 
 def share_rows(first, count, rank, hot_count, plan_ref, rows_ref, outs):
@@ -293,24 +276,31 @@
 def collect_kernel(hot_count, adapter_device, plan_ref, *refs):
     local = refs[:PLANE]
     arrived = refs[PLANE : PLANE + PLANES - 1]
-    out_ref, sems = refs[PLANE + PLANES - 1], refs[-1]
+    out_ref = refs[PLANE + PLANES - 1]
     used = plan_ref[SECTIONS * hot_count]
-
-    def copy_of(at):
-        return lambda source: pltpu.make_async_copy(source, out_ref.at[at], sems.at[at])
-
-    for at in range(hot_count):
-
-        @pl.when(at < used)
+    for place in range(hot_count):
+
+        @pl.when(place < used)
         def _():
-            entry = plan_ref[PLANE_LIST * hot_count + at]
-            start_rows(plan_ref, entry, hot_count, adapter_device, local, arrived, copy_of(at))
-
-    for at in range(hot_count):
-
-        @pl.when(at < used)
-        def _():
-            copy_of(at)(local[0].at[0]).wait()
+            entry = plan_ref[PLANE_LIST * hot_count + place]
+            kind = plan_ref[FROM_KIND * hot_count + entry]
+            slot = plan_ref[FROM_SLOT * hot_count + entry]
+
+            @pl.when(kind == 0)
+            def _():
+                holder = lax.div(slot, adapter_device)
+                inner = slot - holder * adapter_device
+                for at in range(PLANE):
+
+                    @pl.when(holder == at)
+                    def _():
+                        out_ref[place] = local[at][inner]
+
+            for distance in range(1, PLANES):
+
+                @pl.when(kind == distance)
+                def _():
+                    out_ref[place] = arrived[distance - 1][slot]
 
 
 def hot_lanes(first_row, rows, hot_count, plan_ref):
@@ -495,11 +485,9 @@
         + [pl.BlockSpec((block, quarter), lambda at: (at, 0))] * PLANE,
         compiler_params=pltpu.CompilerParams(vmem_limit_bytes=VMEM_LIMIT),
     )(tokens, input_norm_scale.reshape(1, width))
-    base = jnp.dot(normed, key_matrix, preferred_element_type=jnp.float32)
-    cosine, sine = turn_tables(positions)
     second = swap(columns[1], 1, peer_count)
-    plan, base, cosine, sine, slot_index, second = lax.optimization_barrier(
-        (plan, base, cosine, sine, slot_index, second)
+    plan, positions, slot_index, second = lax.optimization_barrier(
+        (plan, positions, slot_index, second)
     )
 
     rest = jax.ShapeDtypeStruct((hot_count - FEW, part, key_width), jnp.bfloat16)
@@ -517,9 +505,8 @@
                     jax.ShapeDtypeStruct((slot, rank + part, quarter), jnp.bfloat16)
                     for slot in slots
                 ],
-                [SMEM] + [ANY] * PLANE,
-                [ANY] * len(slots),
-                [pltpu.SemaphoreType.DMA((sum(slots),))],
+                [SMEM] + [VMEM] * PLANE,
+                [VMEM] * len(slots),
             )(plan, *local)
             *sends, third, fourth = lax.optimization_barrier((*sends, third, fourth))
             arrived = [
@@ -531,9 +518,8 @@
                 functools.partial(collect_kernel, hot_count, adapter_device),
                 [jax.ShapeDtypeStruct((hot_count, rank + part, quarter), jnp.bfloat16)]
                 + ([] if slots[0] == hot_count else [rest] * PLANE),
-                [SMEM] + [ANY] * (PLANE + PLANES - 1),
+                [SMEM] + [VMEM] * (PLANE + PLANES - 1),
                 [VMEM] * (1 if slots[0] == hot_count else 1 + PLANE),
-                [pltpu.SemaphoreType.DMA((hot_count,))],
             )(plan, *local, *arrived)
             if not more:
                 more = share(
@@ -553,17 +539,19 @@
         plan[SECTIONS * hot_count + 1], cases, plan, columns[2], columns[3], *local
     )
 
-    shared = share(
-        call(
-            functools.partial(partial_kernel, rank, hot_count),
-            [jax.ShapeDtypeStruct((FEW + 2, part, key_width), jnp.bfloat16)] * PLANE,
-            [SMEM] + [VMEM] * (1 + PLANE),
-            [VMEM] * PLANE,
-            [pltpu.VMEM((PLANE, rank, rows), jnp.float32)],
-            flops=2 * hot_count * rank * width * rows,
-            bytes_accessed=6 * 1024 * 1024,
-        )(plan, used_rows, columns[0], second, third, fourth)
-    )
+    shared = call(
+        functools.partial(partial_kernel, rank, hot_count),
+        [jax.ShapeDtypeStruct((FEW + 2, part, key_width), jnp.bfloat16)] * PLANE,
+        [SMEM] + [VMEM] * (1 + PLANE),
+        [VMEM] * PLANE,
+        [pltpu.VMEM((PLANE, rank, rows), jnp.float32)],
+        flops=2 * hot_count * rank * width * rows,
+        bytes_accessed=6 * 1024 * 1024,
+    )(plan, used_rows, columns[0], second, third, fourth)
+    normed, positions, own = lax.optimization_barrier((normed, positions, shared[0]))
+    shared = share([own, *shared[1:]])
+    base = jnp.dot(normed, key_matrix, preferred_element_type=jnp.float32)
+    cosine, sine = turn_tables(positions)
     return call(
         functools.partial(finish_kernel, hot_count),
         jax.ShapeDtypeStruct((out_rows, key_width), jnp.bfloat16),

time: 97.7 us -> 99.5 us (1.018)
  waiting for transfers between devices: 24.2 us -> 30.6 us
  other arithmetic: 3.97 us -> 1.29 us
  blocking collectives: 31 us -> 29.1 us
    ppermute x12, waiting for transfers between devices: 24.2 us -> 30.6 us  [swap(): lax.ppermute(value, 'seq', [(i, i ^ distance) for i in range(peer_count)])]
    all_to_all x1, blocking collectives: 31 us -> 29.1 us  [on_device(): lax.all_to_all(outgoing, 'seq', split_axis=0, concat_axis=0, tiled=True)]
    unnamed x21 -> x23, local copies, waits for them, and re-layouts: 6.01 us -> 5.51 us
  transfers between devices with their start and end apart: 12 -> 12, of which waited for: 5 -> 4; matrix products, arithmetic and copies ran while one was open for 11% -> 8% of each run, Pallas kernels for 6% -> 6%
where the time goes in v2:
time: 99.5 us; the launch traced here: 98.7 us
  waiting for transfers between devices  30.6 us (31%)
  blocking collectives  29.1 us (29%)
  Pallas kernels  13 us (13%)
  starting transfers between devices  11.7 us (12%)
  local copies, waits for them, and re-layouts  6.09 us (6%)
  matrix products  5.7 us (6%)
  other arithmetic  1.29 us (1%)
    ppermute x12, waiting for transfers between devices, swap(): lax.ppermute(value, 'seq', [(i, i ^ distance) for i in range(peer_count)])  30.6 us
    all_to_all x1, blocking collectives, on_device(): lax.all_to_all(outgoing, 'seq', split_axis=0, concat_axis=0, tiled=True)  29.1 us
    ppermute x12, starting transfers between devices, swap(): lax.ppermute(value, 'seq', [(i, i ^ distance) for i in range(peer_count)])  11.7 us
    dot_general x1, matrix products, planes_outgoing(): base = jnp.dot(normed, key_matrix, preferred_element_type=jnp.float32)  5.7 us
    unnamed x23, local copies, waits for them, and re-layouts  5.51 us
    pallas_call x1, Pallas kernels, planes_outgoing(): call(functools.partial(finish_kernel, hot_count), jax.ShapeDtypeStruct((o...  2.57 us
    pallas_call x1, Pallas kernels, planes_outgoing(): call(functools.partial(partial_kernel, rank, hot_count), [jax.ShapeDtypeS...  2.51 us
    pallas_call x1, Pallas kernels, run(): call(functools.partial(collect_kernel, hot_count, adapter_device), [jax.S...  2.48 us
  transfers between devices with their start and end apart: 12, of which 4 were waited for; matrix products, arithmetic and copies ran while one was open for 8% of the time, Pallas kernels for 6%

profile of v2, /device:TPU:1, one launch (start us, length us, event | category | flops | bytes accessed | tf_op | source)
XLA Modules:
  0.0 98.7 jit_solution(3574363532431122921)
XLA Ops:
  0.0 1.3 %copy-done.1 = bf16[2,4096,64]{1,2,0:T(8,128)(2,1)S(1)} copy-done((bf16[2,4096,64]{1,2,0:T(8,128)(2,1)S(1)}, bf16[2,4096,64]{1,2,0:T(8,128)(2,1)}, u32[]{:S(2)}) %copy-start.1) | copy-done | bytes 1048600
  1.3 0.9 copy-done.2
  2.2 0.9 shard_map.92
  3.1 0.0 copy-start.10
  3.1 0.1 collective-permute-start.63
  3.3 2.7 %collective-permute-start.65 = (bf16[2,80,1024]{2,1,0:T(8,128)(2,1)}, bf16[2,80,1024]{2,1,0:T(8,128)(2,1)}, u32[]{:S(2)}, u32[]{:S(2)}) collective-permute-start(bf16[2,80,1024]{2,1,0:T(8,128)(2,1)} %get-tuple-element.449), channel_id=1, source_target_pairs={{0,2},{1,3},{2,0},{3,1},{4,6},{5,7},{6,4},{7,5},{8,10},{9,11},{10,... | collective-permute-start | bytes 983048 | tf_op jit(solution)/shard_map/ppermute | solution.py:76
  5.9 0.0 collective-permute-start.66
  6.0 0.2 reduce-window.8
  6.2 2.0 %shard_map.91.plan_ref = s32[99]{0:T(128)S(1)} custom-call(s32[8]{0:T(128)S(1)} %copy-done.6, s32[8]{0:T(128)S(1)} %bitcast.17, s32[8]{0:T(128)S(1)} %copy-done.5), custom_call_target="tpu_custom_call" | custom-call | tf_op jit(solution)/shard_map/pallas_call | solution.py:467
  8.1 0.1 convert_reduce_fusion.1
  8.2 0.0 collective-permute-done.63
  8.2 0.7 copy-done.8
  9.0 1.6 %copy-done = bf16[256,4096]{1,0:T(8,128)(2,1)S(1)} copy-done((bf16[256,4096]{1,0:T(8,128)(2,1)S(1)}, bf16[256,4096]{1,0:T(8,128)(2,1)}, u32[]{:S(2)}) %copy-start) | copy-done | bytes 2097176
  10.5 1.3 %shard_map.93 = (bf16[256,4096]{1,0:T(8,128)(2,1)S(1)}, bf16[256,1024]{1,0:T(8,128)(2,1)S(1)}, bf16[256,1024]{1,0:T(8,128)(2,1)S(1)}, bf16[256,1024]{1,0:T(8,128)(2,1)S(1)}, bf16[256,1024]{1,0:T(8,128)(2,1)S(1)}) custom-call(bf16[256,4096]{1,0:T(8,128)(2,1)S(1)} %copy-done, f32[1,4096]{1,0:T(1,128)S(1)} %bitcast.15), custom_call_target="tpu_custom_call" | custom-call | tf_op jit(solution)/shard_map/pallas_call | solution.py:475
  11.8 0.4 collective-permute-start.64
  12.3 0.1 select_reduce_fusion
  12.3 0.2 convert_reduce_fusion
  12.6 1.2 %collective-permute-done.64.refs_1_ = bf16[256,1024]{1,0:T(8,128)(2,1)S(1)} collective-permute-done((bf16[256,1024]{1,0:T(8,128)(2,1)S(1)}, bf16[256,1024]{1,0:T(8,128)(2,1)S(1)}, u32[]{:S(2)}, u32[]{:S(2)}) %collective-permute-start.64) | collective-permute-done | bytes 524320 | tf_op jit(solution)/shard_map/ppermute | solution.py:76
  13.8 0.6 slice.3
  15.0 0.0 collective-permute-done.65
  15.0 6.3 %collective-permute-done.66 = bf16[2,80,1024]{2,1,0:T(8,128)(2,1)} collective-permute-done((bf16[2,80,1024]{2,1,0:T(8,128)(2,1)S(1)}, bf16[2,80,1024]{2,1,0:T(8,128)(2,1)}, u32[]{:S(2)}, u32[]{:S(2)}) %collective-permute-start.66) | collective-permute-done | bytes 327712 | tf_op jit(solution)/shard_map/ppermute | solution.py:76
  21.3 31.8 %conditional.1 = (bf16[256,1024]{1,0:T(8,128)(2,1)}, bf16[256,1024]{1,0:T(8,128)(2,1)}, bf16[8,80,1024]{2,1,0:T(8,128)(2,1)}, bf16[5,16,1024]{2,1,0:T(8,128)(2,1...) conditional(s32[]{:T(128)} %bitcast.6, (s32[99]{0:T(128)S(1)}, ...), branch_computations={%region_4.5_spmd, %region_5.6_spmd, %region_6.7_spmd, %region_7.8_... | conditional | bytes 21889400 | solution.py:538
  21.3 1.3 %branch_1_fun.2 = (bf16[3,80,1024]{2,1,0:T(8,128)(2,1)S(1)}, bf16[2,80,1024]{2,1,0:T(8,128)(2,1)S(1)}, bf16[1,80,1024]{2,1,0:T(8,128)(2,1)S(1)}) custom-call(s32[99]{0:T(128)S(1)} %get-tuple-element.193.plan_ref, bf16[2,80,1024]{2,1,0:T(8,128)(2,1)S(1)} %get-tuple-element.194.refs_0_, bf16[2,80,1024]{2,1,0:T(8,128)(2,1)S(1)} %get-tuple-element.195.refs_1_, ...), custom_call_target="tpu_custom_call" | custom-call | tf_op jit(solution)/shard_map/cond/branch_1_fun/pallas_call | solution.py:502
  22.6 1.5 %collective-permute-start.5 = (bf16[256,1024]{1,0:T(8,128)(2,1)S(1)}, bf16[256,1024]{1,0:T(8,128)(2,1)}, u32[]{:S(2)}, u32[]{:S(2)}) collective-permute-start(bf16[256,1024]{1,0:T(8,128)(2,1)S(1)} %get-tuple-element.203), channel_id=1, source_target_pairs={{0,2},{1,3},{2,0},{3,1},{4,6},{5,7},{6,4},{7,5},{8,10},{9,11},{10,... | collective-permute-start | bytes 1572872 | tf_op jit(solution)/shard_map/cond/branch_1_fun/ppermute | solution.py:76
  24.1 0.6 collective-permute-start.6
  24.7 1.4 %collective-permute-start.7 = (bf16[3,80,1024]{2,1,0:T(8,128)(2,1)S(1)}, bf16[3,80,1024]{2,1,0:T(8,128)(2,1)S(1)}, u32[]{:S(2)}, u32[]{:S(2)}) collective-permute-start(bf16[3,80,1024]{2,1,0:T(8,128)(2,1)S(1)} %get-tuple-element.205), channel_id=1, source_target_pairs={{0,4},{1,5},{2,6},{3,7},{4,0},{5,1},{6,2},{7,3},{8,12},{9,13},{10,... | collective-permute-start | bytes 1474568 | tf_op jit(solution)/shard_map/cond/branch_1_fun/ppermute | solution.py:76
  26.0 2.3 %collective-permute-start.8 = (bf16[2,80,1024]{2,1,0:T(8,128)(2,1)S(1)}, bf16[2,80,1024]{2,1,0:T(8,128)(2,1)S(1)}, u32[]{:S(2)}, u32[]{:S(2)}) collective-permute-start(bf16[2,80,1024]{2,1,0:T(8,128)(2,1)S(1)} %get-tuple-element.206), channel_id=1, source_target_pairs={{0,8},{1,9},{2,10},{3,11},{4,12},{5,13},{6,14},{7,15},{8,0},{9,1},... | collective-permute-start | bytes 983048 | tf_op jit(solution)/shard_map/cond/branch_1_fun/ppermute | solution.py:76
  28.3 0.0 collective-permute-start.9
  28.3 21.9 %collective-permute-done.9.refs_6_ = bf16[1,80,1024]{2,1,0:T(8,128)(2,1)S(1)} collective-permute-done((bf16[1,80,1024]{2,1,0:T(8,128)(2,1)S(1)}, bf16[1,80,1024]{2,1,0:T(8,128)(2,1)S(1)}, u32[]{:S(2)}, u32[]{:S(2)}) %collective-permute-start.9) | collective-permute-done | bytes 163872 | tf_op jit(solution)/shard_map/cond/branch_1_fun/ppermute | solution.py:76
  50.2 0.0 collective-permute-done.8.refs_5_
  50.2 0.0 collective-permute-done.7.refs_4_
  50.2 2.5 %branch_1_fun.3 = (bf16[8,80,1024]{2,1,0:T(8,128)(2,1)}, bf16[5,16,1024]{2,1,0:T(8,128)(2,1)S(1)}, bf16[5,16,1024]{2,1,0:T(8,128)(2,1)}, bf16[5,16,1024]{2,1,0:T(8,128)(2,1)}, bf16[5,16,1024]{2,1,0:T(8,128)(2,1)}) custom-call(s32[99]{0:T(128)S(1)} %get-tuple-element.193.plan_ref, bf16[2,80,1024]{2,1,0:T(8,128)(2,1)S(1)} %get-tuple-element.194.refs_0_, ...), custom_call_target="tpu_custom_call" | custom-call | tf_op jit(solution)/shard_map/cond/branch_1_fun/pallas_call | solution.py:517
  52.7 0.0 collective-permute-done.5
  52.7 0.0 collective-permute-done.6
  53.1 2.5 %shard_map.94 = (bf16[5,16,1024]{2,1,0:T(8,128)(2,1)S(1)}, bf16[5,16,1024]{2,1,0:T(8,128)(2,1)S(1)}, bf16[5,16,1024]{2,1,0:T(8,128)(2,1)S(1)}, bf16[5,16,1024]{2,1,0:T(8,128)(2,1)S(1)}) custom-call(s32[99]{0:T(128)S(1)} %shard_map.91.plan_ref, bf16[8,80,1024]{2,1,0:T(8,128)(2,1)} %get-tuple-element.453.rows_ref, ...), custom_call_target="tpu_custom_call" | custom-call | flops 1073741824 | bytes 6291456 | tf_op jit(solution)/shard_map/pallas_call | solution.py:542
  55.6 0.9 collective-permute-start.67
  56.6 1.2 %collective-permute-start.68 = (bf16[5,16,1024]{2,1,0:T(8,128)(2,1)S(1)}, bf16[5,16,1024]{2,1,0:T(8,128)(2,1)S(1)}, u32[]{:S(2)}, u32[]{:S(2)}) collective-permute-start(bf16[5,16,1024]{2,1,0:T(8,128)(2,1)S(1)} %get-tuple-element.464), channel_id=1, source_target_pairs={{0,2},{1,3},{2,0},{3,1},{4,6},{5,7},{6,4},{7,5},{8,10},{9,11},{10,... | collective-permute-start | bytes 491528 | tf_op jit(solution)/shard_map/ppermute | solution.py:76
  57.8 0.5 collective-permute-start.69
  58.3 0.5 fusion.1
  58.8 5.7 %fusion.3.base_ref = f32[256,1024]{1,0:T(8,128)S(1)} fusion(bf16[256,4096]{1,0:T(8,128)(2,1)S(1)} %get-tuple-element.459, bf16[4096,1024]{1,0:T(8,128)(2,1)} %param.23), kind=kOutput, calls=%fused_computation.16 | convolution fusion | flops 2147483648 | bytes 11534336 | tf_op jit(solution)/shard_map/dot_general | solution.py:553
  64.5 0.1 pad_maximum_fusion.cosine_ref
  64.6 0.1 pad_maximum_fusion.1.sine_ref
  64.7 0.0 collective-permute-done.67.refs_1_
  64.7 0.0 collective-permute-done.68.refs_2_
  64.7 1.3 %collective-permute-done.69.refs_3_ = bf16[5,16,1024]{2,1,0:T(8,128)(2,1)S(1)} collective-permute-done((bf16[5,16,1024]{2,1,0:T(8,128)(2,1)S(1)}, bf16[5,16,1024]{2,1,0:T(8,128)(2,1)S(1)}, u32[]{:S(2)}, u32[]{:S(2)}) %collective-permute-start.69) | collective-permute-done | bytes 163872 | tf_op jit(solution)/shard_map/ppermute | solution.py:76
  66.0 2.6 %shard_map.95 = bf16[512,1024]{1,0:T(8,128)(2,1)S(1)} custom-call(s32[99]{0:T(128)S(1)} %shard_map.91.plan_ref, f32[256,1024]{1,0:T(8,128)S(1)} %fusion.3.base_ref, f32[256,128]{1,0:T(8,128)S(1)} %pad_maximum_fusion.cosine_ref, f32[256,128]{1,0:T(8,128)S(1)} %pad_maximum_fusion.1.sine_ref, s32[1,256]{1,0:T(1,128)S(1)} %bitcast.16, ...), custom_call_target="tpu_custom_call" | custom-call | flops 536870912 | bytes 6291456 | tf_op jit(solution)/shard_map/pallas_call | solution.py:555
  68.6 29.1 %all_to_all.5 = bf16[16,32,1024]{2,1,0:T(8,128)(2,1)S(1)} all-to-all(bf16[16,32,1024]{2,1,0:T(8,128)(2,1)S(1)} %bitcast.13), channel_id=1, replica_groups=mesh['groups'=2,'seq'=16] {'seq'}, dimensions={0} | all-to-all | bytes 2097152 | tf_op jit(solution)/shard_map/all_to_all | solution.py:670
  97.7 1.0 copy.95
  (22 shorter events, 0.1 us)
Async XLA Ops:
  0.0 6.0 %copy-start.6 = (s32[8]{0:T(128)S(1)}, s32[8]{0:T(128)}, u32[]{:S(2)}) copy-start(s32[8]{0:T(128)} %length_ref.1) | copy-start | bytes 100
  0.0 6.2 %copy-start.4 = (s32[8,1]{0,1:T(1,128)S(1)}, s32[8,1]{0,1:T(1,128)}, u32[]{:S(2)}) copy-start(s32[8,1]{0,1:T(1,128)} %param.27) | copy-start | bytes 100
  0.0 6.2 %copy-start.5 = (s32[8]{0:T(128)S(1)}, s32[8]{0:T(128)}, u32[]{:S(2)}) copy-start(s32[8]{0:T(128)} %id_ref.1) | copy-start | bytes 100
  0.0 1.3 %copy-start.1 = (bf16[2,4096,64]{1,2,0:T(8,128)(2,1)S(1)}, bf16[2,4096,64]{1,2,0:T(8,128)(2,1)}, u32[]{:S(2)}) copy-start(bf16[2,4096,64]{1,2,0:T(8,128)(2,1)} %param.24) | copy-start | bytes 3145732
  1.3 0.9 copy-start.2
  2.2 6.7 %copy-start.3 = (f32[4096]{0:T(1024)S(1)}, f32[4096]{0:T(1024)}, u32[]{:S(2)}) copy-start(f32[4096]{0:T(1024)} %param.22) | copy-start | bytes 49156
  3.1 9.2 %copy-start.10 = (s32[256,1]{0,1:T(1,128)S(1)}, s32[256,1]{0,1:T(1,128)}, u32[]{:S(2)}) copy-start(s32[256,1]{0,1:T(1,128)} %param.29) | copy-start | bytes 3076
  3.1 5.1 %collective-permute-start.63 = (bf16[2,80,1024]{2,1,0:T(8,128)(2,1)S(1)}, bf16[2,80,1024]{2,1,0:T(8,128)(2,1)S(1)}, u32[]{:S(2)}, u32[]{:S(2)}) collective-permute-start(bf16[2,80,1024]{2,1,0:T(8,128)(2,1)S(1)} %get-tuple-element.441), channel_id=1, source_target_pairs={{0,1},{1,0},{2,3},{3,2},{4,5},{5,4},{6,7},{7,6},{8,9},{9,8},{10,11... | collective-permute-start | bytes 983048 | tf_op jit(solution)/shard_map/ppermute | solution.py:76
  3.3 11.7 %collective-permute-start.65 = (bf16[2,80,1024]{2,1,0:T(8,128)(2,1)}, bf16[2,80,1024]{2,1,0:T(8,128)(2,1)}, u32[]{:S(2)}, u32[]{:S(2)}) collective-permute-start(bf16[2,80,1024]{2,1,0:T(8,128)(2,1)} %get-tuple-element.449), channel_id=1, source_target_pairs={{0,2},{1,3},{2,0},{3,1},{4,6},{5,7},{6,4},{7,5},{8,10},{9,11},{10,... | collective-permute-start | bytes 983048 | tf_op jit(solution)/shard_map/ppermute | solution.py:76
  5.9 15.3 %collective-permute-start.66 = (bf16[2,80,1024]{2,1,0:T(8,128)(2,1)S(1)}, bf16[2,80,1024]{2,1,0:T(8,128)(2,1)}, u32[]{:S(2)}, u32[]{:S(2)}) collective-permute-start(bf16[2,80,1024]{2,1,0:T(8,128)(2,1)S(1)} %get-tuple-element.450), channel_id=1, source_target_pairs={{0,3},{1,2},{2,1},{3,0},{4,7},{5,6},{6,5},{7,4},{8,11},{9,10},{10,... | collective-permute-start | bytes 983048 | tf_op jit(solution)/shard_map/ppermute | solution.py:76
  8.2 0.7 copy-start.8
  8.9 1.6 %copy-start = (bf16[256,4096]{1,0:T(8,128)(2,1)S(1)}, bf16[256,4096]{1,0:T(8,128)(2,1)}, u32[]{:S(2)}) copy-start(bf16[256,4096]{1,0:T(8,128)(2,1)} %token_ref) | copy-start | bytes 6291460
  10.5 10.7 %copy-start.7 = (bf16[2,80,1024]{2,1,0:T(8,128)(2,1)S(1)}, bf16[2,80,1024]{2,1,0:T(8,128)(2,1)}, u32[]{:S(2)}) copy-start(bf16[2,80,1024]{2,1,0:T(8,128)(2,1)} %get-tuple-element.447) | copy-start | bytes 983044
  10.5 10.7 %copy-start.9 = (bf16[2,80,1024]{2,1,0:T(8,128)(2,1)S(1)}, bf16[2,80,1024]{2,1,0:T(8,128)(2,1)}, u32[]{:S(2)}) copy-start(bf16[2,80,1024]{2,1,0:T(8,128)(2,1)} %copy-done.8) | copy-start | bytes 983044
  11.8 2.0 %collective-permute-start.64 = (bf16[256,1024]{1,0:T(8,128)(2,1)S(1)}, bf16[256,1024]{1,0:T(8,128)(2,1)S(1)}, u32[]{:S(2)}, u32[]{:S(2)}) collective-permute-start(bf16[256,1024]{1,0:T(8,128)(2,1)S(1)} %get-tuple-element.443), channel_id=1, source_target_pairs={{0,1},{1,0},{2,3},{3,2},{4,5},{5,4},{6,7},{7,6},{8,9},{9,8},{10,11... | collective-permute-start | bytes 1572872 | tf_op jit(solution)/shard_map/ppermute | solution.py:76
  22.6 30.1 %collective-permute-start.5 = (bf16[256,1024]{1,0:T(8,128)(2,1)S(1)}, bf16[256,1024]{1,0:T(8,128)(2,1)}, u32[]{:S(2)}, u32[]{:S(2)}) collective-permute-start(bf16[256,1024]{1,0:T(8,128)(2,1)S(1)} %get-tuple-element.203), channel_id=1, source_target_pairs={{0,2},{1,3},{2,0},{3,1},{4,6},{5,7},{6,4},{7,5},{8,10},{9,11},{10,... | collective-permute-start | bytes 1572872 | tf_op jit(solution)/shard_map/cond/branch_1_fun/ppermute | solution.py:76
  24.1 28.6 %collective-permute-start.6 = (bf16[256,1024]{1,0:T(8,128)(2,1)S(1)}, bf16[256,1024]{1,0:T(8,128)(2,1)}, u32[]{:S(2)}, u32[]{:S(2)}) collective-permute-start(bf16[256,1024]{1,0:T(8,128)(2,1)S(1)} %get-tuple-element.204), channel_id=1, source_target_pairs={{0,3},{1,2},{2,1},{3,0},{4,7},{5,6},{6,5},{7,4},{8,11},{9,10},{10,... | collective-permute-start | bytes 1572872 | tf_op jit(solution)/shard_map/cond/branch_1_fun/ppermute | solution.py:76
  24.7 25.5 %collective-permute-start.7 = (bf16[3,80,1024]{2,1,0:T(8,128)(2,1)S(1)}, bf16[3,80,1024]{2,1,0:T(8,128)(2,1)S(1)}, u32[]{:S(2)}, u32[]{:S(2)}) collective-permute-start(bf16[3,80,1024]{2,1,0:T(8,128)(2,1)S(1)} %get-tuple-element.205), channel_id=1, source_target_pairs={{0,4},{1,5},{2,6},{3,7},{4,0},{5,1},{6,2},{7,3},{8,12},{9,13},{10,... | collective-permute-start | bytes 1474568 | tf_op jit(solution)/shard_map/cond/branch_1_fun/ppermute | solution.py:76
  26.0 24.2 %collective-permute-start.8 = (bf16[2,80,1024]{2,1,0:T(8,128)(2,1)S(1)}, bf16[2,80,1024]{2,1,0:T(8,128)(2,1)S(1)}, u32[]{:S(2)}, u32[]{:S(2)}) collective-permute-start(bf16[2,80,1024]{2,1,0:T(8,128)(2,1)S(1)} %get-tuple-element.206), channel_id=1, source_target_pairs={{0,8},{1,9},{2,10},{3,11},{4,12},{5,13},{6,14},{7,15},{8,0},{9,1},... | collective-permute-start | bytes 983048 | tf_op jit(solution)/shard_map/cond/branch_1_fun/ppermute | solution.py:76
  28.3 21.9 %collective-permute-start.9 = (bf16[1,80,1024]{2,1,0:T(8,128)(2,1)S(1)}, bf16[1,80,1024]{2,1,0:T(8,128)(2,1)S(1)}, u32[]{:S(2)}, u32[]{:S(2)}) collective-permute-start(bf16[1,80,1024]{2,1,0:T(8,128)(2,1)S(1)} %get-tuple-element.207), channel_id=1, source_target_pairs={{0,12},{1,13},{2,14},{3,15},{4,8},{5,9},{6,10},{7,11},{8,4},{9,5},... | collective-permute-start | bytes 491528 | tf_op jit(solution)/shard_map/cond/branch_1_fun/ppermute | solution.py:76
  55.6 9.1 %collective-permute-start.67 = (bf16[5,16,1024]{2,1,0:T(8,128)(2,1)S(1)}, bf16[5,16,1024]{2,1,0:T(8,128)(2,1)S(1)}, u32[]{:S(2)}, u32[]{:S(2)}) collective-permute-start(bf16[5,16,1024]{2,1,0:T(8,128)(2,1)S(1)} %get-tuple-element.463), channel_id=1, source_target_pairs={{0,1},{1,0},{2,3},{3,2},{4,5},{5,4},{6,7},{7,6},{8,9},{9,8},{10,11... | collective-permute-start | bytes 491528 | tf_op jit(solution)/shard_map/ppermute | solution.py:76
  56.6 8.2 %collective-permute-start.68 = (bf16[5,16,1024]{2,1,0:T(8,128)(2,1)S(1)}, bf16[5,16,1024]{2,1,0:T(8,128)(2,1)S(1)}, u32[]{:S(2)}, u32[]{:S(2)}) collective-permute-start(bf16[5,16,1024]{2,1,0:T(8,128)(2,1)S(1)} %get-tuple-element.464), channel_id=1, source_target_pairs={{0,2},{1,3},{2,0},{3,1},{4,6},{5,7},{6,4},{7,5},{8,10},{9,11},{10,... | collective-permute-start | bytes 491528 | tf_op jit(solution)/shard_map/ppermute | solution.py:76
  57.8 8.2 %collective-permute-start.69 = (bf16[5,16,1024]{2,1,0:T(8,128)(2,1)S(1)}, bf16[5,16,1024]{2,1,0:T(8,128)(2,1)S(1)}, u32[]{:S(2)}, u32[]{:S(2)}) collective-permute-start(bf16[5,16,1024]{2,1,0:T(8,128)(2,1)S(1)} %get-tuple-element.465), channel_id=1, source_target_pairs={{0,3},{1,2},{2,1},{3,0},{4,7},{5,6},{6,5},{7,4},{8,11},{9,10},{10,... | collective-permute-start | bytes 491528 | tf_op jit(solution)/shard_map/ppermute | solution.py:76
